TPU v7x, 256 devices: a whole 4x4x8 slice. The times are simulated.
256 devices in a mesh: gz: 8 (over y, x_lo), row: 4 (over x_hi, core), col: 8 (over z).
Axes of the slice: x: 4 (x_hi: 2, x_lo: 2; x = x_hi * 2 + x_lo), y: 4, z: 8, core: 2. Of those that a mesh axis runs over, the one named last changes fastest.
Arguments:
- sections: bfloat16 [16, 2048, 4096], P('gz', 'row', 'col'), may hold values from -6 to 6
Outputs:
- correlation: float32 [16, 2, 16, 32, 1024], P('gz', None, 'row', 'col')
All inputs are finite; a program needn't handle non-finite values.
Results may differ from a plain program's by a relative error of at most 0.011.
Values may be sent and summed in bfloat16 or wider, within the bound.
No kernel may reach another device: no remote copies, remote signals or barrier semaphores. Data moves between devices by JAX's collectives and lax.ppermute only.
A program may use at most 64 MiB of HBM per device.

v0:
```python
import math

import jax
import jax.numpy as jnp
from jax import lax
from jax.sharding import PartitionSpec as P

PATCH = 160
STRIDE = 128
OFF = 32
RIM = 16


full_turn = 2.0 * math.pi


def extended(cells, sides, width):
    for axis, dim in sides:
        count = lax.axis_size(axis)
        ends = count - 1
        head = lax.slice_in_dim(cells, 0, width, axis=dim)
        tail = lax.slice_in_dim(cells, cells.shape[dim] - width, cells.shape[dim], axis=dim)
        cells = jnp.concatenate(
            [
                lax.ppermute(tail, axis, [(i, (i + 1) % count) for i in range(ends)]),
                cells,
                lax.ppermute(head, axis, [((i + 1) % count, i) for i in range(ends)]),
            ],
            axis=dim,
        )
    return cells


def from_behind(value, axis, steps):
    count = lax.axis_size(axis)
    leading, last = (max(0, -steps), min(count, count - steps))
    return lax.ppermute(value, axis, [(source, source + steps) for source in range(leading, last)])


def dft_tables():
    positions = jnp.arange(PATCH, dtype=jnp.int32)
    angles = (positions[:, None] * positions[None, :] % PATCH).astype(jnp.float32) * (
        full_turn / PATCH
    )
    cosine_table = jnp.cos(angles)
    sine_table = jnp.sin(angles)
    forward_cat = jnp.concatenate([cosine_table, -sine_table], axis=1).astype(jnp.bfloat16)
    row_mix = jnp.concatenate(
        [
            jnp.concatenate([cosine_table, sine_table], axis=1),
            jnp.concatenate([-sine_table, cosine_table], axis=1),
        ],
        axis=0,
    ).astype(jnp.bfloat16)
    shifts = jnp.arange(OFF, dtype=jnp.int32) - OFF // 2
    offset_angles = (positions[:, None] * shifts[None, :] % PATCH).astype(jnp.float32) * (
        full_turn / PATCH
    )
    offset_cos = jnp.cos(offset_angles)
    offset_sin = jnp.sin(offset_angles)
    inverse_cat = jnp.concatenate(
        [
            jnp.concatenate([offset_cos, offset_sin], axis=1),
            jnp.concatenate([-offset_sin, offset_cos], axis=1),
        ],
        axis=0,
    ).astype(jnp.bfloat16)
    inverse_rows = jnp.concatenate([offset_cos, -offset_sin], axis=0).astype(jnp.bfloat16)
    return (forward_cat, row_mix, inverse_cat, inverse_rows)


def extract(padded):
    grid_side = (padded.shape[1] - 2 * RIM) // STRIDE
    pieces = []
    for row_index in range(grid_side):
        for col_index in range(grid_side):
            pieces.append(
                padded[
                    :,
                    STRIDE * row_index : STRIDE * row_index + PATCH,
                    STRIDE * col_index : STRIDE * col_index + PATCH,
                ]
            )
    return jnp.stack(pieces, axis=1)


def normalize(patches):
    values = patches.astype(jnp.float32)
    centered = values - jnp.mean(values, axis=(-2, -1), keepdims=True)
    inverse_norm = lax.rsqrt(jnp.mean(centered * centered, axis=(-2, -1), keepdims=True) + 1e-05)
    return (centered * inverse_norm).astype(jnp.bfloat16)


def spectrum(normed, tables):
    forward_cat, row_mix, inverse_cat, inverse_rows = tables
    first = jnp.einsum(
        "spmn,nl->spml", normed, forward_cat, preferred_element_type=jnp.float32
    ).astype(jnp.bfloat16)
    stacked = jnp.concatenate([first[..., :PATCH], first[..., PATCH:]], axis=2)
    return jnp.einsum("km,spml->spkl", row_mix, stacked, preferred_element_type=jnp.float32).astype(
        jnp.bfloat16
    )


def correlate(left_spec, right_spec, tables):
    forward_cat, row_mix, inverse_cat, inverse_rows = tables
    left_real = left_spec[:, :, :PATCH, :].astype(jnp.float32)
    left_imag = left_spec[:, :, PATCH:, :].astype(jnp.float32)
    right_real = right_spec[:, :, :PATCH, :].astype(jnp.float32)
    right_imag = right_spec[:, :, PATCH:, :].astype(jnp.float32)
    cross_real = left_real * right_real + left_imag * right_imag
    cross_imag = left_imag * right_real - left_real * right_imag
    cross = jnp.concatenate([cross_real, cross_imag], axis=-1).astype(jnp.bfloat16)
    half_inverse = jnp.einsum(
        "spkl,lv->spkv", cross, inverse_cat, preferred_element_type=jnp.float32
    ).astype(jnp.bfloat16)
    stacked = jnp.concatenate([half_inverse[..., :OFF], half_inverse[..., OFF:]], axis=2)
    result = jnp.einsum(
        "ku,spkv->spuv", inverse_rows, stacked, preferred_element_type=jnp.float32
    ) * (1.0 / PATCH**3)
    return result.reshape(result.shape[0], result.shape[1], OFF * OFF)


def shards(sections):
    section_count = sections.shape[0]
    grid_side = sections.shape[1] // STRIDE
    tables = dft_tables()
    padded = extended(sections, (("row", 1), ("col", 2)), RIM)
    arriving = from_behind(padded, "gz", -1)
    spectra = spectrum(normalize(extract(jnp.concatenate([padded, arriving], axis=0))), tables)
    current = spectra[:section_count]
    nearer = correlate(current, spectra[1 : section_count + 1], tables)
    farther = correlate(current, spectra[2 : section_count + 2], tables)
    result = jnp.stack([nearer, farther], axis=1)
    return result.reshape(section_count, 2, grid_side, grid_side, OFF * OFF)


def solution(mesh):
    return jax.shard_map(
        shards,
        mesh=mesh,
        in_specs=(P("gz", "row", "col"),),
        out_specs=P("gz", None, "row", "col", None),
        check_vma=False,
    )
```

profile of v0, /device:TPU:1, one launch (start us, length us, event | category | flops | bytes accessed | tf_op | source)
XLA Modules:
  0.0 104.4 jit_solution(14386357629300344865)
XLA Ops:
  0.0 0.8 fusion.89
  0.8 6.0 %collective-permute-start = (bf16[2,16,512]{2,1,0:T(8,128)(2,1)S(1)}, bf16[2,16,512]{2,1,0:T(8,128)(2,1)S(1)}, u32[]{:S(2)}, u32[]{:S(2)}) collective-permute-start(bf16[2,16,512]{2,1,0:T(8,128)(2,1)S(1)} %get-tuple-element.18), channel_id=1, source_target_pairs={{0,8},{8,16},{16,24},{1,9},{9,17},{17,25},{2,10},{10,18},{18,26},{... | collective-permute-start | bytes 98312 | tf_op jit(solution)/shard_map/ppermute | solution.py:25
  6.8 1.9 %collective-permute-start.1 = (bf16[2,16,512]{2,1,0:T(8,128)(2,1)S(1)}, bf16[2,16,512]{2,1,0:T(8,128)(2,1)S(1)}, u32[]{:S(2)}, u32[]{:S(2)}) collective-permute-start(bf16[2,16,512]{2,1,0:T(8,128)(2,1)S(1)} %get-tuple-element.17), channel_id=1, source_target_pairs={{8,0},{16,8},{24,16},{9,1},{17,9},{25,17},{10,2},{18,10},{26,18},{... | collective-permute-start | bytes 98312 | tf_op jit(solution)/shard_map/ppermute | solution.py:27
  8.8 1.3 %constant_dynamic-update-slice_fusion.1 = bf16[2,544,512]{2,1,0:T(8,128)(2,1)S(1)} fusion(bf16[2,544,512]{2,1,0:T(8,128)(2,1)S(1)} %constant_dynamic-update-slice_fusion.2, bf16[2,512,512]{2,1,0:T(8,128)(2,1)} %param.1), kind=kLoop, calls=%fused_computation.108 | loop fusion | bytes 2097152
  10.1 3.5 %collective-permute-done.1 = bf16[2,16,512]{2,1,0:T(8,128)(2,1)S(1)} collective-permute-done((bf16[2,16,512]{2,1,0:T(8,128)(2,1)S(1)}, bf16[2,16,512]{2,1,0:T(8,128)(2,1)S(1)}, u32[]{:S(2)}, u32[]{:S(2)}) %collective-permute-start.1) | collective-permute-done | bytes 32800 | tf_op jit(solution)/shard_map/ppermute | solution.py:27
  13.6 0.1 fusion.86
  13.7 3.6 %collective-permute-start.2 = (bf16[2,544,16]{2,1,0:T(8,128)(2,1)S(1)}, bf16[2,544,16]{2,1,0:T(8,128)(2,1)S(1)}, u32[]{:S(2)}, u32[]{:S(2)}) collective-permute-start(bf16[2,544,16]{2,1,0:T(8,128)(2,1)S(1)} %get-tuple-element.11), channel_id=1, source_target_pairs={{0,1},{1,2},{2,3},{3,4},{4,5},{5,6},{6,7},{8,9},{9,10},{10,11},{11... | collective-permute-start | bytes 104456 | tf_op jit(solution)/shard_map/ppermute | solution.py:25
  17.3 1.3 %collective-permute-start.3 = (bf16[2,544,16]{2,1,0:T(8,128)(2,1)S(1)}, bf16[2,544,16]{2,1,0:T(8,128)(2,1)S(1)}, u32[]{:S(2)}, u32[]{:S(2)}) collective-permute-start(bf16[2,544,16]{2,1,0:T(8,128)(2,1)S(1)} %get-tuple-element.12), channel_id=1, source_target_pairs={{1,0},{2,1},{3,2},{4,3},{5,4},{6,5},{7,6},{9,8},{10,9},{11,10},{12... | collective-permute-start | bytes 104456 | tf_op jit(solution)/shard_map/ppermute | solution.py:27
  18.6 2.2 %collective-permute-done.2 = bf16[2,544,16]{2,1,0:T(8,128)(2,1)S(1)} collective-permute-done((bf16[2,544,16]{2,1,0:T(8,128)(2,1)S(1)}, bf16[2,544,16]{2,1,0:T(8,128)(2,1)S(1)}, u32[]{:S(2)}, u32[]{:S(2)}) %collective-permute-start.2) | collective-permute-done | bytes 34848 | tf_op jit(solution)/shard_map/ppermute | solution.py:25
  20.7 4.0 %collective-permute-done.3 = bf16[2,544,16]{2,1,0:T(8,128)(2,1)S(1)} collective-permute-done((bf16[2,544,16]{2,1,0:T(8,128)(2,1)S(1)}, bf16[2,544,16]{2,1,0:T(8,128)(2,1)S(1)}, u32[]{:S(2)}, u32[]{:S(2)}) %collective-permute-start.3) | collective-permute-done | bytes 34848 | tf_op jit(solution)/shard_map/ppermute | solution.py:27
  24.7 0.8 pad_maximum_fusion.1
  25.6 1.3 %collective-permute-start.4 = (bf16[2,544,544]{2,1,0:T(8,128)(2,1)S(1)}, bf16[2,544,544]{2,1,0:T(8,128)(2,1)S(1)}, u32[]{:S(2)}, u32[]{:S(2)}) collective-permute-start(bf16[2,544,544]{2,1,0:T(8,128)(2,1)S(1)} %pad_maximum_fusion.1), channel_id=1, source_target_pairs={{32,0},{64,32},{96,64},{128,96},{160,128},{192,160},{224,192},{33,... | collective-permute-start | bytes 3551240 | tf_op jit(solution)/shard_map/ppermute | solution.py:37
  26.9 0.6 fusion.68
  27.5 0.7 negate_convert_fusion
  28.2 0.2 fusion.77
  28.5 29.4 %collective-permute-done.4 = bf16[2,544,544]{2,1,0:T(8,128)(2,1)S(1)} collective-permute-done((bf16[2,544,544]{2,1,0:T(8,128)(2,1)S(1)}, bf16[2,544,544]{2,1,0:T(8,128)(2,1)S(1)}, u32[]{:S(2)}, u32[]{:S(2)}) %collective-permute-start.4) | collective-permute-done | bytes 1183776 | tf_op jit(solution)/shard_map/ppermute | solution.py:37
  57.8 1.0 pad_maximum_fusion
  59.4 1.0 convert_reduce_fusion
  60.4 1.7 %fusion.2 = f32[4,16]{0,1:T(8,128)S(1)} fusion(bf16[4,16,160,160]{3,2,0,1:T(8,128)(2,1)S(1)} %fusion.41, f32[4,16]{0,1:T(8,128)S(1)} %broadcast_multiply_fusion), kind=kLoop, calls=%fused_computation.4 | loop fusion | flops 6553536 | bytes 3277312 | tf_op jit(solution)/shard_map/reduce_sum | solution.py:90
  62.1 5.1 %convolution_convert_fusion = bf16[4,16,160,320]{3,2,1,0:T(8,128)(2,1)} fusion(bf16[160,160]{1,0:T(8,128)(2,1)S(1)} %get-tuple-element.22, bf16[160,160]{1,0:T(8,128)(2,1)S(1)} %get-tuple-element.23, bf16[4,16,160,160]{3,2,0,1:T(8,128)(2,1)S(1)} %fusion.41, f32[4,16]{0,1:T(8,128)S(1)} %add_rsqrt_fusion, f32[4,16]{0,1:T(8,128)S(1)} %broadcast_multiply_fusion), kind=kOutput, calls=%fused_computation.19 | convolution fusion | flops 1058611200 | bytes 9933312 | tf_op jit(solution)/shard_map/spmn,nl->spml/dot_general | solution.py:96
  67.2 11.2 %fusion.85 = (bf16[4,16,160,160]{3,2,1,0:T(8,128)(2,1)}, bf16[4,16,160,160]{3,2,1,0:T(8,128)(2,1)}) fusion(bf16[4,16,160,320]{3,2,1,0:T(8,128)(2,1)} %convolution_convert_fusion), kind=kLoop, calls=%fused_computation.130 | loop fusion | bytes 13107200 | tf_op jit(solution)/shard_map/slice | solution.py:99
  78.4 9.5 %convert_bitcast_fusion = bf16[4,16,320,160]{2,3,1,0:T(8,128)(2,1)S(1)} fusion(bf16[4,16,160,160]{3,2,1,0:T(8,128)(2,1)} %get-tuple-element.10, bf16[4,16,160,160]{3,2,1,0:T(8,128)(2,1)} %get-tuple-element.9, bf16[160,160]{1,0:T(8,128)(2,1)S(1)} %get-tuple-element.23, bf16[160,160]{1,0:T(8,128)(2,1)S(1)} %get-tuple-element.22, bf16[160,160]{1,0:T(8,128)(2,1)S(1)} %fusion.68), kind=kOutput, calls=%fused_computation.18 | convolution fusion | flops 2114355200 | bytes 13260800 | tf_op jit(solution)/shard_map/km,spml->spkl/dot_general | solution.py:100
  87.9 7.3 %fusion.11 = (bf16[2,16,160,160]{2,3,1,0:T(8,128)(2,1)S(1)}, bf16[2,16,160,160]{2,3,1,0:T(8,128)(2,1)S(1)}, bf16[2,16,160,160]{2,3,1,0:T(8,128)(2,1)S(1)}, bf16[2,16,160,160]{2,3,1,0:T(8,128)(2,1)}) fusion(bf16[4,16,320,160]{2,3,1,0:T(8,128)(2,1)S(1)} %convert_bitcast_fusion), kind=kLoop, calls=%fused_computation.21 | loop fusion | flops 18022400 | bytes 16384000 | tf_op jit(solution)/shard_map/convert.10
  95.2 1.5 %fusion.30 = bf16[2,16,160,64]{2,3,1,0:T(8,128)(2,1)S(1)} fusion(bf16[2,16,160,160]{2,3,1,0:T(8,128)(2,1)S(1)} %get-tuple-element.7, bf16[2,16,160,160]{2,3,1,0:T(8,128)(2,1)S(1)} %get-tuple-element.5, bf16[160,32]{0,1:T(8,128)(2,1)S(1)} %get-tuple-element.21, bf16[160,32]{0,1:T(8,128)(2,1)S(1)} %get-tuple-element.20, bf16[160,32]{0,1:T(8,128)(2,1)S(1)} %get-tuple-element.19), kind=kOutput, calls=%fused_computation.39 | convolution fusion | flops 216760320 | bytes 3962880 | tf_op jit(solution)/shard_map/spkl,lv->spkv/dot_general | solution.py:114
  96.9 0.4 fusion.34
  97.3 1.0 copy.9
  98.3 1.3 %stack.75 = f32[2,1,4,4,1024]{4,3,2,0,1:T(4,128)S(1)} reshape(f32[2,16,32,32]{3,2,1,0:T(8,128)} %copy.9) | data formatting | bytes 262144 | tf_op jit(solution)/shard_map/stack | solution.py:134
  99.6 2.9 %fusion.27 = bf16[2,16,160,64]{2,3,1,0:T(8,128)(2,1)S(1)} fusion(bf16[2,16,160,160]{2,3,1,0:T(8,128)(2,1)} %get-tuple-element.8, bf16[2,16,160,160]{2,3,1,0:T(8,128)(2,1)S(1)} %get-tuple-element.6, bf16[160,32]{0,1:T(8,128)(2,1)S(1)} %get-tuple-element.21, bf16[160,32]{0,1:T(8,128)(2,1)S(1)} %get-tuple-element.20, bf16[160,32]{0,1:T(8,128)(2,1)S(1)} %get-tuple-element.19), kind=kOutput, calls=%fused_computation.38 | convolution fusion | flops 216760320 | bytes 3962880 | tf_op jit(solution)/shard_map/spkl,lv->spkv/dot_general | solution.py:114
  102.7 0.4 fusion.33
  103.1 0.2 copy.11
  103.3 0.3 stack.76
  103.6 0.7 copy.12
  (25 shorter events, 0.6 us)
Async XLA Ops:
  0.8 8.0 %collective-permute-start = (bf16[2,16,512]{2,1,0:T(8,128)(2,1)S(1)}, bf16[2,16,512]{2,1,0:T(8,128)(2,1)S(1)}, u32[]{:S(2)}, u32[]{:S(2)}) collective-permute-start(bf16[2,16,512]{2,1,0:T(8,128)(2,1)S(1)} %get-tuple-element.18), channel_id=1, source_target_pairs={{0,8},{8,16},{16,24},{1,9},{9,17},{17,25},{2,10},{10,18},{18,26},{... | collective-permute-start | bytes 98312 | tf_op jit(solution)/shard_map/ppermute | solution.py:25
  6.8 6.7 %collective-permute-start.1 = (bf16[2,16,512]{2,1,0:T(8,128)(2,1)S(1)}, bf16[2,16,512]{2,1,0:T(8,128)(2,1)S(1)}, u32[]{:S(2)}, u32[]{:S(2)}) collective-permute-start(bf16[2,16,512]{2,1,0:T(8,128)(2,1)S(1)} %get-tuple-element.17), channel_id=1, source_target_pairs={{8,0},{16,8},{24,16},{9,1},{17,9},{25,17},{10,2},{18,10},{26,18},{... | collective-permute-start | bytes 98312 | tf_op jit(solution)/shard_map/ppermute | solution.py:27
  13.7 7.0 %collective-permute-start.2 = (bf16[2,544,16]{2,1,0:T(8,128)(2,1)S(1)}, bf16[2,544,16]{2,1,0:T(8,128)(2,1)S(1)}, u32[]{:S(2)}, u32[]{:S(2)}) collective-permute-start(bf16[2,544,16]{2,1,0:T(8,128)(2,1)S(1)} %get-tuple-element.11), channel_id=1, source_target_pairs={{0,1},{1,2},{2,3},{3,4},{4,5},{5,6},{6,7},{8,9},{9,10},{10,11},{11... | collective-permute-start | bytes 104456 | tf_op jit(solution)/shard_map/ppermute | solution.py:25
  17.3 7.5 %collective-permute-start.3 = (bf16[2,544,16]{2,1,0:T(8,128)(2,1)S(1)}, bf16[2,544,16]{2,1,0:T(8,128)(2,1)S(1)}, u32[]{:S(2)}, u32[]{:S(2)}) collective-permute-start(bf16[2,544,16]{2,1,0:T(8,128)(2,1)S(1)} %get-tuple-element.12), channel_id=1, source_target_pairs={{1,0},{2,1},{3,2},{4,3},{5,4},{6,5},{7,6},{9,8},{10,9},{11,10},{12... | collective-permute-start | bytes 104456 | tf_op jit(solution)/shard_map/ppermute | solution.py:27
  25.6 32.2 %collective-permute-start.4 = (bf16[2,544,544]{2,1,0:T(8,128)(2,1)S(1)}, bf16[2,544,544]{2,1,0:T(8,128)(2,1)S(1)}, u32[]{:S(2)}, u32[]{:S(2)}) collective-permute-start(bf16[2,544,544]{2,1,0:T(8,128)(2,1)S(1)} %pad_maximum_fusion.1), channel_id=1, source_target_pairs={{32,0},{64,32},{96,64},{128,96},{160,128},{192,160},{224,192},{33,... | collective-permute-start | bytes 3551240 | tf_op jit(solution)/shard_map/ppermute | solution.py:37
where the time goes:
time: 106 us; the launch traced here: 104 us
  waiting for transfers between devices  39 us (37%)
  matrix products  19.9 us (19%)
  local copies, waits for them, and re-layouts  17.5 us (17%)
  starting transfers between devices  14.1 us (13%)
  other arithmetic  13.6 us (13%)
    ppermute x1, waiting for transfers between devices, from_behind(): lax.ppermute(value, axis, [(source, source + steps) for source in range(l...  29.4 us
    slice x1, local copies, waits for them, and re-layouts, spectrum(): stacked = jnp.concatenate([first[..., :PATCH], first[..., PATCH:]], axis=2)  11.2 us
    ppermute x2, starting transfers between devices, extended(): lax.ppermute(tail, axis, [(i, (i + 1) % count) for i in range(ends)])  9.59 us
    dot_general x1, matrix products, spectrum(): jnp.einsum('km,spml->spkl', row_mix, stacked, preferred_element_type=jnp....  9.48 us
    another operation x4, other arithmetic  8.87 us
    ppermute x2, waiting for transfers between devices, extended(): lax.ppermute(head, axis, [((i + 1) % count, i) for i in range(ends)])  7.49 us
    dot_general x1, matrix products, spectrum(): jnp.einsum('spmn,nl->spml', normed, forward_cat, preferred_element_type=j...  5.11 us
    dot_general x2, matrix products, correlate(): jnp.einsum('spkl,lv->spkv', cross, inverse_cat, preferred_element_type=jn...  4.48 us
  transfers between devices with their start and end apart: 5, of which 4 were waited for; matrix products, arithmetic and copies ran while one was open for 3% of the time, Pallas kernels for 0%

commit v1 on v0

v1 whole, which is shorter than its diff:
```python
import functools
import math

import jax
import jax.numpy as jnp
import numpy as np
from jax import lax
from jax.experimental import pallas as pl
from jax.experimental.pallas import tpu as pltpu
from jax.sharding import PartitionSpec as P

PATCH = 160
STRIDE = 128
OFF = 32
RIM = 16
HALF = PATCH // 2
AXES = ("gz", "row", "col")


def tables():
    turn = 2.0 * math.pi / PATCH
    bf = lambda a: np.asarray(a, np.float32).astype(jnp.bfloat16)
    q = np.full(256, -1)
    q[:128] = np.arange(128) + RIM
    q[128 : 128 + RIM] = np.arange(RIM) + 128 + RIM
    q[256 - RIM :] = np.arange(RIM)
    l = np.arange(HALF + 1)
    ang = (q[:, None] * l[None, :] % PATCH) * turn
    live = (q >= 0)[:, None]
    columns = np.zeros((256, 256))
    columns[:, : HALF + 1] = np.where(live, np.cos(ang), 0.0)
    columns[:, 128 : 128 + HALF + 1] = np.where(live, -np.sin(ang), 0.0)
    k = np.arange(HALF)
    m = np.arange(PATCH)
    ang = (k[:, None] * m[None, :] % PATCH) * turn
    sines = np.sin(ang)
    sines[0] = np.where(m % 2 == 0, 1.0, -1.0)
    rows = np.concatenate([np.cos(ang), sines], axis=0)
    place = np.arange(OFF)
    u = (place % 8) * 4 + place // 8
    ang = ((u - OFF // 2)[:, None] * k[None, :] % PATCH) * turn
    sines = np.sin(ang)
    sines[:, 0] = np.where(u % 2 == 0, 1.0, -1.0)
    back_rows = np.concatenate([np.cos(ang), sines], axis=1)
    v = np.arange(OFF) - OFF // 2
    ang = (l[:, None] * v[None, :] % PATCH) * turn
    weight = np.where((l == 0) | (l == HALF), 1.0, 2.0)[:, None]
    one = np.zeros((256, OFF))
    one[: HALF + 1] = np.cos(ang)
    one[128 : 128 + HALF + 1] = -np.sin(ang)
    one = bf(one).astype(np.float32)
    one[: HALF + 1] *= weight
    one[128 : 128 + HALF + 1] *= weight
    back_columns = np.zeros((4, 256, 128))
    for s in range(4):
        back_columns[s, :, s * OFF : (s + 1) * OFF] = one
    return bf(columns), bf(rows), bf(back_rows), bf(back_columns.reshape(1024, 128))


def spectra_of(blocks, rim, columns, rows, live, which):
    lane = lax.broadcasted_iota(jnp.int32, (PATCH, 128), 1)
    head = lane < RIM
    tail = lane >= 128 - RIM
    side_lanes = head | tail
    top = lax.broadcasted_iota(jnp.int32, (HALF, 128), 0) == 0
    normed = []
    for j in which:
        before = blocks[j - 1] if j > 0 else rim
        behind = blocks[j + 1] if j < 3 else rim
        main = blocks[j]
        side = jnp.where(head, behind, jnp.where(tail, before, 0.0))
        mean = jnp.sum(main + side, keepdims=True) * (1.0 / PATCH**2)
        main = main - mean
        side = jnp.where(side_lanes, side - mean, 0.0)
        variance = jnp.sum(main * main + side * side, keepdims=True) * (1.0 / PATCH**2)
        scale = lax.rsqrt(variance + 1e-05)
        if live is not None:
            scale = scale * live
        normed.append(
            jnp.concatenate([(main * scale).astype(jnp.bfloat16), (side * scale).astype(jnp.bfloat16)], axis=1)
        )
    first = jnp.dot(
        jnp.concatenate(normed, axis=0), columns, preferred_element_type=jnp.float32
    ).astype(jnp.bfloat16)
    result = []
    for n in range(len(which)):
        mixed = jnp.dot(rows, first[PATCH * n : PATCH * (n + 1)], preferred_element_type=jnp.float32)
        cos_real, cos_imag = mixed[:HALF, :128], mixed[:HALF, 128:]
        sin_real, sin_imag = mixed[HALF:, :128], mixed[HALF:, 128:]
        plus = [
            jnp.where(top, cos_real, cos_real + sin_imag),
            jnp.where(top, cos_imag, cos_imag - sin_real),
        ]
        minus = [
            jnp.where(top, sin_real, cos_real - sin_imag),
            jnp.where(top, sin_imag, cos_imag + sin_real),
        ]
        real = jnp.concatenate([plus[0], minus[0]], axis=0)
        imag = jnp.concatenate([plus[1], minus[1]], axis=0)
        result.append(jnp.concatenate([real, imag], axis=1).astype(jnp.bfloat16))
    return result


def half_back(left, right, back_rows):
    top = lax.broadcasted_iota(jnp.int32, (HALF, 128), 0) == 0
    left = left.astype(jnp.float32)
    right = right.astype(jnp.float32)
    lr, li, rr, ri = left[:, :128], left[:, 128:], right[:, :128], right[:, 128:]
    real = lr * rr + li * ri
    imag = li * rr - lr * ri
    pr, mr, p_i, mi = real[:HALF], real[HALF:], imag[:HALF], imag[HALF:]
    even = [jnp.where(top, pr, pr + mr), jnp.where(top, p_i, p_i + mi)]
    odd = [jnp.where(top, mr, mi - p_i), jnp.where(top, mi, pr - mr)]
    real = jnp.concatenate([even[0], odd[0]], axis=0)
    imag = jnp.concatenate([even[1], odd[1]], axis=0)
    both = jnp.concatenate([real, imag], axis=1).astype(jnp.bfloat16)
    return jnp.dot(back_rows, both, preferred_element_type=jnp.float32)


def kernel(fresh, kept, pairs, earlier, keep, *refs):
    refs = list(refs)
    live_ref = refs.pop(0)
    padded_ref, rims_ref = refs.pop(0), refs.pop(0)
    kept_ref = refs.pop(0) if kept else None
    earlier_refs = [refs.pop(0) for _ in range(len(earlier))]
    columns_ref, rows_ref, back_rows_ref, back_columns_ref = [refs.pop(0) for _ in range(4)]
    out_ref = refs.pop(0)
    spectra_ref = refs.pop(0) if keep else None
    rim_scr, line_scr = refs
    i = pl.program_id(0)
    tall = rims_ref.shape[-1]

    @pl.when(i == 0)
    def _():
        for s in range(fresh):
            both = rims_ref[s].astype(jnp.float32)
            wide = jnp.concatenate(
                [both[RIM:], jnp.zeros((128 - 2 * RIM, tall), jnp.float32), both[:RIM]], axis=0
            )
            rim_scr[s] = wide.T

    live = live_ref[0] if live_ref is not None else None
    start = pl.multiple_of(i * STRIDE, STRIDE)
    columns, rows = columns_ref[...], rows_ref[...]
    back_rows, back_columns = back_rows_ref[...], back_columns_ref[...]
    spectra = {}
    for s in range(fresh):
        blocks = [
            padded_ref[s, pl.ds(start, PATCH), 128 * b : 128 * (b + 1)].astype(jnp.float32)
            for b in range(4)
        ]
        rim = rim_scr[s, pl.ds(start, PATCH), :]
        spectra[kept + s] = spectra_of(blocks, rim, columns, rows, live, range(4))
        if keep:
            for j in range(4):
                spectra_ref[s, 0, j] = spectra[kept + s][j]
    pieces = []
    for a, b in pairs:
        for j in range(4):
            left = kept_ref[a, 0, j] if a < kept else spectra[a][j]
            right = kept_ref[b, 0, j] if b < kept else spectra[b][j]
            halves = half_back(left, right, back_rows)
            pieces.append(jnp.concatenate([halves[8 * s : 8 * (s + 1)] for s in range(4)], axis=1))
    lines = jnp.concatenate(pieces, axis=0).astype(jnp.bfloat16)
    line_scr[...] = jnp.dot(lines, back_columns, preferred_element_type=jnp.float32) * (
        1.0 / PATCH**3
    )
    base = 0
    for ref in earlier_refs:
        for n in range(ref.shape[0]):
            out_ref[base] = ref[n]
            base += 1
    for n in range(len(pairs)):
        for b in range(8):
            out_ref[base + n, 0, :, 128 * b : 128 * (b + 1)] = line_scr[pl.ds(32 * n + b, 4, stride=8), :]


def stage(padded, rims, kept, pairs, earlier, keep, live, consts):
    fresh = padded.shape[0]
    side = (padded.shape[1] - 2 * RIM) // STRIDE
    held = 0 if kept is None else kept.shape[0]
    whole = lambda a: pl.BlockSpec(a.shape, lambda i: (0,) * a.ndim)
    operands, specs = [live, padded, rims], [
        pl.BlockSpec(memory_space=pltpu.SMEM),
        whole(padded),
        whole(rims),
    ]
    if held:
        operands.append(kept)
        specs.append(pl.BlockSpec((held, 1, 4, PATCH, 256), lambda i: (0, i, 0, 0, 0)))
    for e in earlier:
        operands.append(e)
        specs.append(pl.BlockSpec((e.shape[0], 1, 4, 1024), lambda i: (0, i, 0, 0)))
    for c in consts:
        operands.append(c)
        specs.append(whole(c))
    total = len(pairs) + sum(e.shape[0] for e in earlier)
    out_shape = [jax.ShapeDtypeStruct((total, side, 4, 1024), jnp.float32)]
    out_specs = [pl.BlockSpec((total, 1, 4, 1024), lambda i: (0, i, 0, 0))]
    if keep:
        out_shape.append(jax.ShapeDtypeStruct((fresh, side, 4, PATCH, 256), jnp.bfloat16))
        out_specs.append(pl.BlockSpec((fresh, 1, 4, PATCH, 256), lambda i: (0, i, 0, 0, 0)))
    flops = 2 * side * 4 * (fresh * (PATCH * 65536 + PATCH**2 * 256) + len(pairs) * 64 * PATCH * 256)
    return pl.pallas_call(
        functools.partial(kernel, fresh, held, pairs, earlier, keep),
        grid=(side,),
        in_specs=specs,
        out_specs=out_specs,
        out_shape=out_shape,
        scratch_shapes=[
            pltpu.VMEM((fresh, rims.shape[-1], 128), jnp.float32),
            pltpu.VMEM((32 * len(pairs), 128), jnp.float32),
        ],
        compiler_params=pltpu.CompilerParams(vmem_limit_bytes=40 * 1024 * 1024),
        cost_estimate=pl.CostEstimate(flops=4 * flops, bytes_accessed=padded.size * 2, transcendentals=0),
    )(*operands)


def ring(value, axis, steps):
    count = lax.axis_size(axis)
    return lax.ppermute(value, axis, [(n, (n + steps) % count) for n in range(count)])


def shards(sections):
    consts = [jnp.asarray(t) for t in tables()]
    height = sections.shape[1]
    row, col, gz = lax.axis_index("row"), lax.axis_index("col"), lax.axis_index("gz")
    rows, cols, blocks = lax.axis_size("row"), lax.axis_size("col"), lax.axis_size("gz")
    above = jnp.where(row > 0, ring(sections[:, height - RIM :], "row", 1), 0)
    below = jnp.where(row < rows - 1, ring(sections[:, :RIM], "row", -1), 0)
    padded = jnp.concatenate([above, sections, below], axis=1)
    arriving = [ring(padded[n : n + 1], "gz", -1) for n in range(2)]
    tall = height + 2 * RIM
    fill = ((0, 0), (0, 0), (0, -tall % 128))
    left = jnp.where(col > 0, ring(jnp.swapaxes(padded[:, :, -RIM:], 1, 2), "col", 1), 0)
    right = jnp.where(col < cols - 1, ring(jnp.swapaxes(padded[:, :, :RIM], 1, 2), "col", -1), 0)
    rims = jnp.pad(jnp.concatenate([left, right], axis=1), fill)
    far_rims = ring(rims, "gz", -1)
    one = jnp.ones((1,), jnp.float32)
    live = (gz < blocks - 1).astype(jnp.float32).reshape(1)
    near, spectra = stage(padded, rims, None, [(0, 1)], [], True, one, consts)
    middle, = stage(arriving[0], far_rims[:1], spectra, [(0, 2), (1, 2)], [], False, live, consts)
    result, = stage(arriving[1], far_rims[1:], spectra, [(1, 2)], [near, middle], False, live, consts)
    return result.reshape(2, 2, result.shape[1], 4, OFF * OFF)


def solution(mesh):
    return jax.shard_map(
        shards,
        mesh=mesh,
        in_specs=(P("gz", "row", "col"),),
        out_specs=P("gz", None, "row", "col", None),
        check_vma=False,
    )
```

time: 106 us -> 64.4 us (0.61)
  the two profiles are of different devices: /device:TPU:1 before, /device:TPU:30 now
where the time goes in v1:
time: 64.4 us; the launch traced here: 64.2 us
  waiting for transfers between devices  24.8 us (39%)
  Pallas kernels  21.6 us (34%)
  starting transfers between devices  10.2 us (16%)
  local copies, waits for them, and re-layouts  6.59 us (10%)
  other arithmetic  0.86 us (1%)
    ppermute x7, waiting for transfers between devices, ring(): lax.ppermute(value, axis, [(n, (n + steps) % count) for n in range(count)])  24.8 us
    pallas_call x3, Pallas kernels, stage(): pl.pallas_call(functools.partial(kernel, fresh, held, pairs, earlier, kee...  21.6 us
    ppermute x7, starting transfers between devices, ring(): lax.ppermute(value, axis, [(n, (n + steps) % count) for n in range(count)])  10.2 us
    slice x3, local copies, waits for them, and re-layouts, shards(): arriving = [ring(padded[n:n + 1], 'gz', -1) for n in range(2)]  3.35 us
    unnamed x9, local copies, waits for them, and re-layouts  1.51 us
  transfers between devices with their start and end apart: 7, of which 3 were waited for; matrix products, arithmetic and copies ran while one was open for 9% of the time, Pallas kernels for 23%

profile of v1, /device:TPU:30, one launch (start us, length us, event | category | flops | bytes accessed | tf_op | source)
XLA Modules:
  0.0 64.2 jit_solution(6384087958425486030)
XLA Ops:
  0.0 0.8 %fusion.4 = (bf16[2,16,512]{2,1,0:T(8,128)(2,1)S(1)}, bf16[2,16,512]{2,1,0:T(8,128)(2,1)S(1)}) fusion(bf16[2,512,512]{2,1,0:T(8,128)(2,1)} %param.5), kind=kLoop, calls=%fused_computation.12 | loop fusion | bytes 131072 | tf_op jit(solution)/shard_map/slice | solution.py:229
  0.8 0.2 copy.13
  1.0 0.9 %collective-permute-start.1 = (bf16[2,16,512]{1,2,0:T(8,128)(2,1)S(1)}, bf16[2,16,512]{1,2,0:T(8,128)(2,1)S(1)}, u32[]{:S(2)}, u32[]{:S(2)}) collective-permute-start(bf16[2,16,512]{1,2,0:T(8,128)(2,1)S(1)} %copy.13), channel_id=1, source_target_pairs={{0,24},{8,0},{16,8},{24,16},{1,25},{9,1},{17,9},{25,17},{2,26},{10... | collective-permute-start | bytes 98312 | tf_op jit(solution)/shard_map/ppermute | solution.py:221
  1.9 0.2 copy.12
  2.1 0.1 collective-permute-start
  2.1 1.5 %copy.14 = bf16[2,512,512]{1,2,0:T(8,128)(2,1)S(1)} copy(bf16[2,512,512]{2,1,0:T(8,128)(2,1)} %param.5) | data formatting | bytes 2097152 | tf_op args[0]
  3.7 3.0 %collective-permute-done.1 = bf16[2,16,512]{1,2,0:T(8,128)(2,1)S(1)} collective-permute-done((bf16[2,16,512]{1,2,0:T(8,128)(2,1)S(1)}, bf16[2,16,512]{1,2,0:T(8,128)(2,1)S(1)}, u32[]{:S(2)}, u32[]{:S(2)}) %collective-permute-start.1) | collective-permute-done | bytes 32800 | tf_op jit(solution)/shard_map/ppermute | solution.py:221
  6.7 4.4 %collective-permute-done = bf16[2,16,512]{1,2,0:T(8,128)(2,1)S(1)} collective-permute-done((bf16[2,16,512]{1,2,0:T(8,128)(2,1)S(1)}, bf16[2,16,512]{1,2,0:T(8,128)(2,1)S(1)}, u32[]{:S(2)}, u32[]{:S(2)}) %collective-permute-start) | collective-permute-done | bytes 32800 | tf_op jit(solution)/shard_map/ppermute | solution.py:221
  11.2 0.8 %pad_maximum_fusion = bf16[2,544,512]{1,2,0:T(8,128)(2,1)S(1)} fusion(bf16[2,16,512]{1,2,0:T(8,128)(2,1)S(1)} %broadcast_select_fusion, bf16[2,512,512]{1,2,0:T(8,128)(2,1)S(1)} %copy.14, bf16[2,16,512]{1,2,0:T(8,128)(2,1)S(1)} %broadcast_select_fusion.1), kind=kLoop, calls=%fused_computation | loop fusion | flops 3342336 | bytes 2228224 | tf_op jit(solution)/shard_map/concatenate | solution.py:231
  12.0 2.0 %collective-permute-start.3 = (bf16[2,16,544]{2,1,0:T(8,128)(2,1)S(1)}, bf16[2,16,544]{2,1,0:T(8,128)(2,1)S(1)}, u32[]{:S(2)}, u32[]{:S(2)}) collective-permute-start(bf16[2,16,544]{2,1,0:T(8,128)(2,1)S(1)} %get-tuple-element.11), channel_id=1, source_target_pairs={{0,1},{1,2},{2,3},{3,4},{4,5},{5,6},{6,7},{7,0},{8,9},{9,10},{10,1... | collective-permute-start | bytes 104456 | tf_op jit(solution)/shard_map/ppermute | solution.py:221
  14.0 1.0 %fusion.3 = (bf16[1,544,512]{1,2,0:T(8,128)(2,1)}, bf16[1,544,512]{1,2,0:T(8,128)(2,1)S(1)}) fusion(bf16[2,544,512]{1,2,0:T(8,128)(2,1)S(1)} %pad_maximum_fusion), kind=kLoop, calls=%fused_computation.11 | loop fusion | bytes 2228224 | tf_op jit(solution)/shard_map/slice | solution.py:232
  14.9 0.6 copy.16.refs_1_
  15.5 4.0 %collective-permute-start.4 = (bf16[2,16,544]{2,1,0:T(8,128)(2,1)S(1)}, bf16[2,16,544]{2,1,0:T(8,128)(2,1)S(1)}, u32[]{:S(2)}, u32[]{:S(2)}) collective-permute-start(bf16[2,16,544]{2,1,0:T(8,128)(2,1)S(1)} %get-tuple-element.12), channel_id=1, source_target_pairs={{0,7},{1,0},{2,1},{3,2},{4,3},{5,4},{6,5},{7,6},{8,15},{9,8},{10,9... | collective-permute-start | bytes 104456 | tf_op jit(solution)/shard_map/ppermute | solution.py:221
  19.6 0.0 copy-start
  19.6 0.0 copy-start.1
  19.6 2.2 %copy.17 = bf16[1,544,512]{2,1,0:T(8,128)(2,1)} copy(bf16[1,544,512]{1,2,0:T(8,128)(2,1)} %get-tuple-element.9) | data formatting | bytes 1114112 | tf_op jit(solution)/shard_map/slice | solution.py:232
  21.7 0.2 copy.15
  22.0 0.9 %collective-permute-start.2 = (bf16[1,544,512]{2,1,0:T(8,128)(2,1)S(1)}, bf16[1,544,512]{2,1,0:T(8,128)(2,1)S(1)}, u32[]{:S(2)}, u32[]{:S(2)}) collective-permute-start(bf16[1,544,512]{2,1,0:T(8,128)(2,1)S(1)} %copy.15), channel_id=1, source_target_pairs={{0,224},{32,0},{64,32},{96,64},{128,96},{160,128},{192,160},{224,1... | collective-permute-start | bytes 1671176 | tf_op jit(solution)/shard_map/ppermute | solution.py:221
  22.9 1.4 %collective-permute-start.6 = (bf16[1,544,512]{2,1,0:T(8,128)(2,1)}, bf16[1,544,512]{2,1,0:T(8,128)(2,1)S(1)}, u32[]{:S(2)}, u32[]{:S(2)}) collective-permute-start(bf16[1,544,512]{2,1,0:T(8,128)(2,1)} %copy.17), channel_id=1, source_target_pairs={{0,224},{32,0},{64,32},{96,64},{128,96},{160,128},{192,160},{224,1... | collective-permute-start | bytes 1671176 | tf_op jit(solution)/shard_map/ppermute | solution.py:221
  24.3 0.0 collective-permute-done.3
  24.3 0.0 collective-permute-done.4
  24.3 0.9 %collective-permute-start.5 = (bf16[2,32,640]{2,1,0:T(8,128)(2,1)S(1)}, bf16[2,32,640]{2,1,0:T(8,128)(2,1)S(1)}, u32[]{:S(2)}, u32[]{:S(2)}) collective-permute-start(bf16[2,32,640]{2,1,0:T(8,128)(2,1)S(1)} %fusion.2.refs_2_), channel_id=1, source_target_pairs={{0,224},{32,0},{64,32},{96,64},{128,96},{160,128},{192,160},{224,1... | collective-permute-start | bytes 245768 | tf_op jit(solution)/shard_map/ppermute | solution.py:221
  25.2 0.0 copy-done
  25.2 0.0 copy-done.1
  25.2 0.0 copy-done.2
  25.2 0.0 copy-done.3
  25.3 8.6 %shard_map.55 = (f32[1,4,4,1024]{3,2,1,0:T(4,128)S(1)}, bf16[2,4,4,160,256]{4,3,2,1,0:T(8,128)(2,1)S(1)}) custom-call(f32[1]{0:T(128)} %constant.29.clone.1.refs_0_, bf16[2,544,512]{2,1,0:T(8,128)(2,1)S(1)} %copy.16.refs_1_, bf16[2,32,640]{2,1,0:T(8,128)(2,1)S(1)} %fusion.2.refs_2_, bf16[256,256]{1,0:T(8,128)(2,1)S(1)} %copy-done.1, ...), custom_call_target="tpu_custom_call" | custom-call | flops 4697620480 | bytes 1114112 | tf_op jit(solution)/shard_map/pallas_call | solution.py:204
  33.8 17.4 %collective-permute-done.5 = bf16[2,32,640]{2,1,0:T(8,128)(2,1)S(1)} collective-permute-done((bf16[2,32,640]{2,1,0:T(8,128)(2,1)S(1)}, bf16[2,32,640]{2,1,0:T(8,128)(2,1)S(1)}, u32[]{:S(2)}, u32[]{:S(2)}) %collective-permute-start.5) | collective-permute-done | bytes 81952 | tf_op jit(solution)/shard_map/ppermute | solution.py:221
  51.2 0.0 collective-permute-done.6.refs_1_
  51.2 6.3 %shard_map.56.refs_5_ = f32[2,4,4,1024]{3,2,1,0:T(4,128)S(1)} custom-call(f32[1]{0:T(128)} %bitcast.refs_0_, bf16[1,544,512]{2,1,0:T(8,128)(2,1)S(1)} %collective-permute-done.6.refs_1_, bf16[1,32,640]{2,1,0:T(8,128)(2,1)S(1)} %get-tuple-element.15.refs_2_, bf16[2,4,4,160,256]{4,3,2,1,0:T(8,128)(2,1)S(1)} %get-tuple-element.7.refs_3_, ...), custom_call_target="tpu_custom_call" | custom-call | flops 2852126720 | bytes 557056 | tf_op jit(solution)/shard_map/pallas_call | solution.py:204
  57.5 0.0 collective-permute-done.2.refs_1_
  57.5 6.7 %shard_map.57 = f32[4,4,4,1024]{3,2,1,0:T(4,128)} custom-call(f32[1]{0:T(128)} %bitcast.refs_0_, bf16[1,544,512]{2,1,0:T(8,128)(2,1)S(1)} %collective-permute-done.2.refs_1_, bf16[1,32,640]{2,1,0:T(8,128)(2,1)S(1)} %get-tuple-element.16.refs_2_, bf16[2,4,4,160,256]{4,3,2,1,0:T(8,128)(2,1)S(1)} %get-tuple-element.7.refs_3_, ...), custom_call_target="tpu_custom_call" | custom-call | flops 2516582400 | bytes 557056 | tf_op jit(solution)/shard_map/pallas_call | solution.py:204
  (9 shorter events, 0.1 us)
Async XLA Ops:
  1.0 5.8 %collective-permute-start.1 = (bf16[2,16,512]{1,2,0:T(8,128)(2,1)S(1)}, bf16[2,16,512]{1,2,0:T(8,128)(2,1)S(1)}, u32[]{:S(2)}, u32[]{:S(2)}) collective-permute-start(bf16[2,16,512]{1,2,0:T(8,128)(2,1)S(1)} %copy.13), channel_id=1, source_target_pairs={{0,24},{8,0},{16,8},{24,16},{1,25},{9,1},{17,9},{25,17},{2,26},{10... | collective-permute-start | bytes 98312 | tf_op jit(solution)/shard_map/ppermute | solution.py:221
  2.1 9.1 %collective-permute-start = (bf16[2,16,512]{1,2,0:T(8,128)(2,1)S(1)}, bf16[2,16,512]{1,2,0:T(8,128)(2,1)S(1)}, u32[]{:S(2)}, u32[]{:S(2)}) collective-permute-start(bf16[2,16,512]{1,2,0:T(8,128)(2,1)S(1)} %copy.12), channel_id=1, source_target_pairs={{0,8},{8,16},{16,24},{24,0},{1,9},{9,17},{17,25},{25,1},{2,10},{10... | collective-permute-start | bytes 98312 | tf_op jit(solution)/shard_map/ppermute | solution.py:221
  12.0 12.3 %collective-permute-start.3 = (bf16[2,16,544]{2,1,0:T(8,128)(2,1)S(1)}, bf16[2,16,544]{2,1,0:T(8,128)(2,1)S(1)}, u32[]{:S(2)}, u32[]{:S(2)}) collective-permute-start(bf16[2,16,544]{2,1,0:T(8,128)(2,1)S(1)} %get-tuple-element.11), channel_id=1, source_target_pairs={{0,1},{1,2},{2,3},{3,4},{4,5},{5,6},{6,7},{7,0},{8,9},{9,10},{10,1... | collective-permute-start | bytes 104456 | tf_op jit(solution)/shard_map/ppermute | solution.py:221
  15.5 8.7 %collective-permute-start.4 = (bf16[2,16,544]{2,1,0:T(8,128)(2,1)S(1)}, bf16[2,16,544]{2,1,0:T(8,128)(2,1)S(1)}, u32[]{:S(2)}, u32[]{:S(2)}) collective-permute-start(bf16[2,16,544]{2,1,0:T(8,128)(2,1)S(1)} %get-tuple-element.12), channel_id=1, source_target_pairs={{0,7},{1,0},{2,1},{3,2},{4,3},{5,4},{6,5},{7,6},{8,15},{9,8},{10,9... | collective-permute-start | bytes 104456 | tf_op jit(solution)/shard_map/ppermute | solution.py:221
  19.6 5.7 %copy-start = (bf16[1024,128]{1,0:T(8,128)(2,1)S(1)}, bf16[1024,128]{1,0:T(8,128)(2,1)}, u32[]{:S(2)}) copy-start(bf16[1024,128]{1,0:T(8,128)(2,1)} %constant.33.clone.refs_6_.refs_7_.refs_9_) | copy-start | bytes 786436
  19.6 5.7 %copy-start.1 = (bf16[256,256]{1,0:T(8,128)(2,1)S(1)}, bf16[256,256]{1,0:T(8,128)(2,1)}, u32[]{:S(2)}) copy-start(bf16[256,256]{1,0:T(8,128)(2,1)} %constant.30.clone.refs_3_.refs_4_.refs_6_) | copy-start | bytes 393220
  19.6 5.7 %copy-start.2 = (bf16[160,160]{1,0:T(8,128)(2,1)S(1)}, bf16[160,160]{1,0:T(8,128)(2,1)}, u32[]{:S(2)}) copy-start(bf16[160,160]{1,0:T(8,128)(2,1)} %constant.31.clone.refs_4_.refs_5_.refs_7_) | copy-start | bytes 153604
  19.6 5.7 %copy-start.3 = (bf16[32,160]{1,0:T(8,128)(2,1)S(1)}, bf16[32,160]{1,0:T(8,128)(2,1)}, u32[]{:S(2)}) copy-start(bf16[32,160]{1,0:T(8,128)(2,1)} %constant.32.clone.refs_5_.refs_6_.refs_8_) | copy-start | bytes 30724
  22.0 35.5 %collective-permute-start.2 = (bf16[1,544,512]{2,1,0:T(8,128)(2,1)S(1)}, bf16[1,544,512]{2,1,0:T(8,128)(2,1)S(1)}, u32[]{:S(2)}, u32[]{:S(2)}) collective-permute-start(bf16[1,544,512]{2,1,0:T(8,128)(2,1)S(1)} %copy.15), channel_id=1, source_target_pairs={{0,224},{32,0},{64,32},{96,64},{128,96},{160,128},{192,160},{224,1... | collective-permute-start | bytes 1671176 | tf_op jit(solution)/shard_map/ppermute | solution.py:221
  22.9 28.3 %collective-permute-start.6 = (bf16[1,544,512]{2,1,0:T(8,128)(2,1)}, bf16[1,544,512]{2,1,0:T(8,128)(2,1)S(1)}, u32[]{:S(2)}, u32[]{:S(2)}) collective-permute-start(bf16[1,544,512]{2,1,0:T(8,128)(2,1)} %copy.17), channel_id=1, source_target_pairs={{0,224},{32,0},{64,32},{96,64},{128,96},{160,128},{192,160},{224,1... | collective-permute-start | bytes 1671176 | tf_op jit(solution)/shard_map/ppermute | solution.py:221
  24.3 26.8 %collective-permute-start.5 = (bf16[2,32,640]{2,1,0:T(8,128)(2,1)S(1)}, bf16[2,32,640]{2,1,0:T(8,128)(2,1)S(1)}, u32[]{:S(2)}, u32[]{:S(2)}) collective-permute-start(bf16[2,32,640]{2,1,0:T(8,128)(2,1)S(1)} %fusion.2.refs_2_), channel_id=1, source_target_pairs={{0,224},{32,0},{64,32},{96,64},{128,96},{160,128},{192,160},{224,1... | collective-permute-start | bytes 245768 | tf_op jit(solution)/shard_map/ppermute | solution.py:221

commit v2 on v1

v2 whole, which is shorter than its diff:
```python
import functools
import math

import jax
import jax.numpy as jnp
import numpy as np
from jax import lax
from jax.experimental import pallas as pl
from jax.experimental.pallas import tpu as pltpu
from jax.sharding import PartitionSpec as P

PATCH = 160
STRIDE = 128
OFF = 32
CUT = 272
STAGE_COST = 30
EDGES_COST = 10_000_000_000
RIM = 16
HALF = PATCH // 2
AXES = ("gz", "row", "col")


def tables():
    turn = 2.0 * math.pi / PATCH
    bf = lambda a: np.asarray(a, np.float32).astype(jnp.bfloat16)
    q = np.full(256, -1)
    q[:128] = np.arange(128) + RIM
    q[128 : 128 + RIM] = np.arange(RIM) + 128 + RIM
    q[256 - RIM :] = np.arange(RIM)
    l = np.arange(HALF + 1)
    ang = (q[:, None] * l[None, :] % PATCH) * turn
    live = (q >= 0)[:, None]
    columns = np.zeros((256, 256))
    columns[:, : HALF + 1] = np.where(live, np.cos(ang), 0.0)
    columns[:, 128 : 128 + HALF + 1] = np.where(live, -np.sin(ang), 0.0)
    k = np.arange(HALF)
    m = np.arange(PATCH)
    ang = (k[:, None] * m[None, :] % PATCH) * turn
    sines = np.sin(ang)
    sines[0] = np.where(m % 2 == 0, 1.0, -1.0)
    rows = np.concatenate([np.cos(ang), sines], axis=0)
    place = np.arange(OFF)
    u = (place % 8) * 4 + place // 8
    ang = ((u - OFF // 2)[:, None] * k[None, :] % PATCH) * turn
    sines = np.sin(ang)
    sines[:, 0] = np.where(u % 2 == 0, 1.0, -1.0)
    back_rows = np.concatenate([np.cos(ang), sines], axis=1)
    v = np.arange(OFF) - OFF // 2
    ang = (l[:, None] * v[None, :] % PATCH) * turn
    weight = np.where((l == 0) | (l == HALF), 1.0, 2.0)[:, None]
    one = np.zeros((256, OFF))
    one[: HALF + 1] = np.cos(ang)
    one[128 : 128 + HALF + 1] = -np.sin(ang)
    one = bf(one).astype(np.float32)
    one[: HALF + 1] *= weight
    one[128 : 128 + HALF + 1] *= weight
    back_columns = np.zeros((4, 256, 128))
    for s in range(4):
        back_columns[s, :, s * OFF : (s + 1) * OFF] = one
    return bf(columns), bf(rows), bf(back_rows), bf(back_columns.reshape(1024, 128))


def total(a):
    a = jnp.sum(a.reshape(PATCH // 8, 8, 128), axis=0)
    return jnp.sum(jnp.sum(a, axis=1, keepdims=True), axis=0, keepdims=True)


def with_top(special, rest):
    top = lax.broadcasted_iota(jnp.int32, (8, 128), 0) == 0
    return jnp.concatenate([jnp.where(top, special[:8], rest[:8]), rest[8:]], axis=0)


def spectra_of(blocks, rim, columns, rows, live):
    lane = lax.broadcasted_iota(jnp.int32, (PATCH, 128), 1)
    head = lane < RIM
    tail = lane >= 128 - RIM
    side_lanes = head | tail
    result = []
    for j in range(4):
        before = blocks[j - 1] if j > 0 else rim
        behind = blocks[j + 1] if j < 3 else rim
        main = blocks[j]
        side = jnp.where(head, behind, jnp.where(tail, before, 0.0))
        mean = total(main + side) * (1.0 / PATCH**2)
        main = main - mean
        side = jnp.where(side_lanes, side - mean, 0.0)
        scale = lax.rsqrt(total(main * main + side * side) * (1.0 / PATCH**2) + 1e-05)
        if live is not None:
            scale = scale * live
        normed = jnp.concatenate(
            [(main * scale).astype(jnp.bfloat16), (side * scale).astype(jnp.bfloat16)], axis=1
        )
        first = jnp.dot(normed, columns, preferred_element_type=jnp.float32).astype(jnp.bfloat16)
        mixed = jnp.dot(rows, first, preferred_element_type=jnp.float32)
        cos_real, cos_imag = mixed[:HALF, :128], mixed[:HALF, 128:]
        sin_real, sin_imag = mixed[HALF:, :128], mixed[HALF:, 128:]
        plus = [with_top(cos_real, cos_real + sin_imag), with_top(cos_imag, cos_imag - sin_real)]
        minus = [with_top(sin_real, cos_real - sin_imag), with_top(sin_imag, cos_imag + sin_real)]
        both = [jnp.concatenate(plus, axis=1), jnp.concatenate(minus, axis=1)]
        result.append(jnp.concatenate(both, axis=0).astype(jnp.bfloat16))
    return result


def half_back(left, right, back_rows):
    left = left.astype(jnp.float32)
    right = right.astype(jnp.float32)
    lr, li, rr, ri = left[:, :128], left[:, 128:], right[:, :128], right[:, 128:]
    real = lr * rr + li * ri
    imag = li * rr - lr * ri
    pr, mr, p_i, mi = real[:HALF], real[HALF:], imag[:HALF], imag[HALF:]
    even = [with_top(pr, pr + mr), with_top(p_i, p_i + mi)]
    odd = [with_top(mr, mi - p_i), with_top(mi, pr - mr)]
    both = [jnp.concatenate(even, axis=1), jnp.concatenate(odd, axis=1)]
    both = jnp.concatenate(both, axis=0).astype(jnp.bfloat16)
    return jnp.dot(back_rows, both, preferred_element_type=jnp.float32)


def edges_kernel(flags_ref, first_ref, last_ref, above_ref, below_ref, low_ref, high_ref):
    up = (flags_ref[0] > 0).astype(jnp.float32)
    down = (flags_ref[1] > 0).astype(jnp.float32)
    for s in range(2):
        for block, ref, take in ((0, low_ref, 0), (1, high_ref, 128 - RIM)):
            tile = (first_ref, last_ref)[block][s].astype(jnp.float32)
            lanes = slice(0, 128) if block == 0 else slice(384, 512)
            top = above_ref[s, :, lanes].astype(jnp.float32) * up
            bottom = below_ref[s, :, lanes].astype(jnp.float32) * down
            tall = jnp.concatenate([top, tile, bottom, jnp.zeros((96, 128), jnp.float32)], axis=0)
            ref[s] = tall.T[take : take + RIM].astype(jnp.bfloat16)


def rims_kernel(flags_ref, above_ref, below_ref, left_ref, right_ref, rims_ref):
    for n, ref in enumerate((above_ref, below_ref, left_ref, right_ref)):
        keep = (flags_ref[n] > 0).astype(jnp.float32)
        part = (ref[...].astype(jnp.float32) * keep).astype(jnp.bfloat16)
        if n < 2:
            rims_ref[:, RIM * n : RIM * (n + 1), :512] = part
            rims_ref[:, RIM * n : RIM * (n + 1), 512:] = jnp.zeros((2, RIM, 128), jnp.bfloat16)
        else:
            rims_ref[:, RIM * n : RIM * (n + 1), :] = part


def kernel(plan, *refs):
    fresh, kept, pairs, at, keep, masked, cuts, span = plan
    refs = list(refs)
    flags_ref = refs.pop(0)
    tile_refs = [refs.pop(0) for _ in cuts]
    rims_ref = refs.pop(0)
    kept_ref = refs.pop(0) if kept else None
    if at:
        refs.pop(0)
    columns_ref, rows_ref, back_rows_ref, back_columns_ref = [refs.pop(0) for _ in range(4)]
    out_ref = refs.pop(0)
    spectra_ref = refs.pop(0)
    rim_scr, half_scr, line_scr, wide_scr, sem = refs
    live = (flags_ref[4] > 0).astype(jnp.float32) if masked else None
    columns, rows = columns_ref[...], rows_ref[...]
    back_rows, back_columns = back_rows_ref[...], back_columns_ref[...]
    for n, s in enumerate(fresh):
        both = rims_ref[s, 2 * RIM :].astype(jnp.float32)
        gap = jnp.zeros((128 - 2 * RIM, both.shape[1]), jnp.float32)
        rim_scr[n] = jnp.concatenate([both[RIM:], gap, both[:RIM]], axis=0).T
    for i in range(*span):
        for n, s in enumerate(fresh):
            blocks = []
            low, high = STRIDE * i - RIM, STRIDE * (i + 1) + RIM
            for b in range(4):
                lanes = slice(128 * b, 128 * (b + 1))
                parts = []
                if low < 0:
                    parts.append(rims_ref[s, :RIM, lanes])
                for ref, start in zip(tile_refs, cuts):
                    begin, end = max(low, start), min(high, start + ref.shape[1])
                    if begin < end:
                        parts.append(ref[n, begin - start : end - start, lanes])
                if high > 512:
                    parts.append(rims_ref[s, RIM : 2 * RIM, lanes])
                parts = [part.astype(jnp.float32) for part in parts]
                blocks.append(jnp.concatenate(parts, axis=0) if len(parts) > 1 else parts[0])
            rim = rim_scr[n, STRIDE * i : STRIDE * i + PATCH, :]
            for j, one in enumerate(spectra_of(blocks, rim, columns, rows, live)):
                spectra_ref[n, i - span[0], j] = one
    tall = 32 * (span[1] - span[0])
    for i in range(*span):
        for n, (a, b) in enumerate(pairs):
            for j in range(4):
                left = kept_ref[a, i, j] if a < kept else spectra_ref[a - kept, i - span[0], j]
                right = kept_ref[b, i, j] if b < kept else spectra_ref[b - kept, i - span[0], j]
                halves = half_back(left, right, back_rows)
                place = tall * n + 32 * (i - span[0]) + 8 * j
                for t in range(4):
                    half_scr[place : place + 8, 256 * t : 256 * (t + 1)] = halves[8 * t : 8 * (t + 1)]
    line_scr[...] = jnp.dot(
        half_scr[...].astype(jnp.bfloat16), back_columns, preferred_element_type=jnp.float32
    ) * (1.0 / PATCH**3)
    for n in range(len(pairs)):
        for i in range(span[1] - span[0]):
            for b in range(8):
                wide_scr[n, i, :, 128 * b : 128 * (b + 1)] = line_scr[
                    pl.ds(tall * n + 32 * i + b, 4, stride=8), :
                ]
    copy = pltpu.make_async_copy(
        wide_scr, out_ref.at[pl.ds(at, len(pairs)), pl.ds(span[0], span[1] - span[0])], sem
    )
    copy.start()
    copy.wait()


IN_VMEM = pl.BlockSpec(memory_space=pltpu.VMEM)
IN_SMEM = pl.BlockSpec(memory_space=pltpu.SMEM)
ANYWHERE = pl.BlockSpec(memory_space=pl.ANY)
PARAMS = pltpu.CompilerParams(vmem_limit_bytes=24 * 1024 * 1024)


def stage(flags, tiles, rims, kept, earlier, consts, fresh, pairs, at, keep, masked, span=(0, 4)):
    held = 0 if kept is None else kept.shape[0]
    operands, aliases = [flags, *tiles.values(), rims], {}
    specs = [IN_SMEM] + [IN_VMEM] * (len(tiles) + 1)
    if held:
        operands.append(kept)
        specs.append(IN_VMEM)
    if earlier is not None:
        aliases[len(operands)] = 0
        operands.append(earlier)
        specs.append(ANYWHERE)
    operands += consts
    specs += [IN_VMEM] * len(consts)
    out_shape = [jax.ShapeDtypeStruct((4, 4, 4, 1024), jnp.float32)]
    out_specs = [ANYWHERE]
    if keep:
        out_shape.append(jax.ShapeDtypeStruct((len(fresh), 4, 4, PATCH, 256), jnp.bfloat16))
        out_specs.append(IN_VMEM)
    height = span[1] - span[0]
    flops = 2 * 4 * height * (len(fresh) * (PATCH * 65536 + PATCH**2 * 256) + len(pairs) * 64 * PATCH * 256)
    return pl.pallas_call(
        functools.partial(kernel, (fresh, held, pairs, at, keep, masked, tuple(tiles), span)),
        in_specs=specs,
        out_specs=out_specs,
        out_shape=out_shape,
        input_output_aliases=aliases,
        scratch_shapes=([] if keep else [pltpu.VMEM((len(fresh), height, 4, PATCH, 256), jnp.bfloat16)])
        + [
            pltpu.VMEM((len(fresh), rims.shape[-1], 128), jnp.float32),
            pltpu.VMEM((32 * height * len(pairs), 1024), jnp.float32),
            pltpu.VMEM((32 * height * len(pairs), 128), jnp.float32),
            pltpu.VMEM((len(pairs), height, 4, 1024), jnp.float32),
            pltpu.SemaphoreType.DMA,
        ],
        compiler_params=PARAMS,
        cost_estimate=pl.CostEstimate(flops=STAGE_COST * flops, bytes_accessed=1 << 20, transcendentals=0),
    )(*operands)


def ring(value, axis, steps):
    count = lax.axis_size(axis)
    return lax.ppermute(value, axis, [(n, (n + steps) % count) for n in range(count)])


def shards(sections):
    consts = [jnp.asarray(t) for t in tables()]
    height, width = sections.shape[1:]
    row, col, gz = lax.axis_index("row"), lax.axis_index("col"), lax.axis_index("gz")
    rows, cols, depth = lax.axis_size("row"), lax.axis_size("col"), lax.axis_size("gz")
    flags = jnp.stack([row > 0, row < rows - 1, col > 0, col < cols - 1, gz < depth - 1]).astype(jnp.int32)
    above = ring(sections[:, height - RIM :], "row", 1)
    below = ring(sections[:, :RIM], "row", -1)
    first = ring(sections[:1], "gz", -1)
    upper = ring(sections[1:, :CUT], "gz", -1)
    blocks = lax.optimization_barrier((sections[:, :, :128], sections[:, :, width - 128 :]))

    def around(operands):
        flags, first_block, last_block, above, below = operands
        edge = jax.ShapeDtypeStruct((2, RIM, 640), jnp.bfloat16)
        low, high = pl.pallas_call(
            edges_kernel,
            in_specs=[IN_SMEM] + [IN_VMEM] * 4,
            out_specs=[IN_VMEM, IN_VMEM],
            out_shape=[edge, edge],
            compiler_params=PARAMS,
            cost_estimate=pl.CostEstimate(flops=EDGES_COST, bytes_accessed=1 << 20, transcendentals=0),
        )(flags, first_block, last_block, above, below)
        left = ring(high, "col", 1)
        right = ring(low, "col", -1)
        rims = pl.pallas_call(
            rims_kernel,
            in_specs=[IN_SMEM] + [IN_VMEM] * 4,
            out_specs=IN_VMEM,
            out_shape=jax.ShapeDtypeStruct((2, 4 * RIM, 640), jnp.bfloat16),
            compiler_params=PARAMS,
        )(flags, above, below, left, right)
        return rims

    rims = lax.cond(
        jnp.sum(flags) < 99,
        around,
        lambda operands: jnp.zeros((2, 4 * RIM, 640), jnp.bfloat16),
        (flags, *blocks, above, below),
    )
    far = ring(rims, "gz", -1)
    result, spectra = stage(flags, {0: sections}, rims, None, None, consts, (0, 1), [(0, 1)], 0, True, False)
    later, spectra = lax.optimization_barrier((sections, spectra))
    lower = ring(later[1:, CUT:], "gz", -1)
    result, = stage(flags, {0: first}, far, spectra, result, consts, (0,), [(0, 2), (1, 2)], 1, False, True)
    result, = stage(
        flags, {0: upper}, far, spectra, result, consts, (1,), [(1, 2)], 3, False, True, (0, 2)
    )
    both = {0: upper, CUT: lower}
    result, = stage(flags, both, far, spectra, result, consts, (1,), [(1, 2)], 3, False, True, (2, 4))
    return result.reshape(2, 2, 4, 4, OFF * OFF)


def solution(mesh):
    return jax.shard_map(
        shards,
        mesh=mesh,
        in_specs=(P("gz", "row", "col"),),
        out_specs=P("gz", None, "row", "col", None),
        check_vma=False,
    )
```

time: 64.4 us -> 42 us (0.65)
  the two profiles are of different devices: /device:TPU:30 before, /device:TPU:96 now
where the time goes in v2:
time: 42 us; the launch traced here: 41.7 us
  Pallas kernels  16.4 us (39%)
  starting transfers between devices  13.6 us (32%)
  waiting for transfers between devices  5.22 us (12%)
  local copies, waits for them, and re-layouts  4.76 us (11%)
  between operations  0.94 us (2%)
  other arithmetic  0.66 us (2%)
    pallas_call x4, Pallas kernels, stage(): pl.pallas_call(functools.partial(kernel, (fresh, held, pairs, at, keep, m...  14.6 us
    ppermute x8, starting transfers between devices, ring(): lax.ppermute(value, axis, [(n, (n + steps) % count) for n in range(count)])  13.6 us
    ppermute x8, waiting for transfers between devices, ring(): lax.ppermute(value, axis, [(n, (n + steps) % count) for n in range(count)])  5.22 us
    slice x1, local copies, waits for them, and re-layouts, shards(): sections[:, :, width - 128:]  1.78 us
    pallas_call x1, Pallas kernels, around(): pl.pallas_call(edges_kernel, in_specs=[IN_SMEM] + [IN_VMEM] * 4, out_spec...  1.27 us
    slice x1, local copies, waits for them, and re-layouts, shards(): first = ring(sections[:1], 'gz', -1)  1.08 us
    slice x1, local copies, waits for them, and re-layouts, shards(): upper = ring(sections[1:, :CUT], 'gz', -1)  0.97 us
  transfers between devices with their start and end apart: 8, of which 2 were waited for; matrix products, arithmetic and copies ran while one was open for 11% of the time, Pallas kernels for 33%

profile of v2, /device:TPU:96, one launch (start us, length us, event | category | flops | bytes accessed | tf_op | source)
XLA Modules:
  0.0 41.7 jit_solution(2945525855314563213)
XLA Ops:
  0.0 0.8 %fusion = (bf16[2,16,512]{2,1,0:T(8,128)(2,1)S(1)}, bf16[2,16,512]{2,1,0:T(8,128)(2,1)S(1)}) fusion(bf16[2,512,512]{2,1,0:T(8,128)(2,1)} %refs_1_.1), kind=kLoop, calls=%fused_computation.1 | loop fusion | bytes 131072 | tf_op jit(solution)/shard_map/slice | solution.py:265
  0.8 0.0 collective-permute-start.3
  0.8 3.2 %collective-permute-start.4 = (bf16[2,16,512]{2,1,0:T(8,128)(2,1)S(1)}, bf16[2,16,512]{2,1,0:T(8,128)(2,1)S(1)}, u32[]{:S(2)}, u32[]{:S(2)}) collective-permute-start(bf16[2,16,512]{2,1,0:T(8,128)(2,1)S(1)} %get-tuple-element.37), channel_id=1, source_target_pairs={{0,24},{8,0},{16,8},{24,16},{1,25},{9,1},{17,9},{25,17},{2,26},{10... | collective-permute-start | bytes 98312 | tf_op jit(solution)/shard_map/ppermute | solution.py:255
  4.0 1.1 %slice.27 = bf16[1,512,512]{2,1,0:T(8,128)(2,1)S(1)} slice(bf16[2,512,512]{2,1,0:T(8,128)(2,1)} %refs_1_.1), slice={[0:1], [0:512], [0:512]} | slice | bytes 1048576 | tf_op jit(solution)/shard_map/slice | solution.py:266
  5.1 4.0 %collective-permute-start.7 = (bf16[1,512,512]{2,1,0:T(8,128)(2,1)S(1)}, bf16[1,512,512]{2,1,0:T(8,128)(2,1)S(1)}, u32[]{:S(2)}, u32[]{:S(2)}) collective-permute-start(bf16[1,512,512]{2,1,0:T(8,128)(2,1)S(1)} %slice.27), channel_id=1, source_target_pairs={{0,224},{32,0},{64,32},{96,64},{128,96},{160,128},{192,160},{224,1... | collective-permute-start | bytes 1572872 | tf_op jit(solution)/shard_map/ppermute | solution.py:255
  9.1 1.0 %slice.21 = bf16[1,272,512]{2,1,0:T(8,128)(2,1)S(1)} slice(bf16[2,512,512]{2,1,0:T(8,128)(2,1)} %refs_1_.1), slice={[1:2], [0:272], [0:512]} | slice | bytes 557056 | tf_op jit(solution)/shard_map/slice | solution.py:267
  10.1 0.6 %collective-permute-start.2 = (bf16[1,272,512]{2,1,0:T(8,128)(2,1)S(1)}, bf16[1,272,512]{2,1,0:T(8,128)(2,1)S(1)}, u32[]{:S(2)}, u32[]{:S(2)}) collective-permute-start(bf16[1,272,512]{2,1,0:T(8,128)(2,1)S(1)} %slice.21), channel_id=1, source_target_pairs={{0,224},{32,0},{64,32},{96,64},{128,96},{160,128},{192,160},{224,1... | collective-permute-start | bytes 835592 | tf_op jit(solution)/shard_map/ppermute | solution.py:255
  10.7 1.8 %fusion.1 = (bf16[2,512,128]{2,1,0:T(8,128)(2,1)S(1)}, bf16[2,512,128]{2,1,0:T(8,128)(2,1)}) fusion(bf16[2,512,512]{2,1,0:T(8,128)(2,1)} %refs_1_.1), kind=kLoop, calls=%fused_computation.2 | loop fusion | bytes 1048576 | tf_op jit(solution)/shard_map/slice | solution.py:268
  12.5 0.1 stack.23
  12.6 0.7 %convert_reduce_fusion = s32[]{:T(128)} fusion(pred[5]{0:T(512)(128)(4,1)S(1)} %stack.23), kind=kLoop, calls=%fused_computation | loop fusion | flops 9 | bytes 9 | tf_op jit(solution)/shard_map/reduce_sum | solution.py:293
  13.9 0.0 collective-permute-done.3
  13.9 0.0 collective-permute-done.4
  13.9 0.0 copy-start
  13.9 0.0 copy-start.1
  13.9 0.0 copy-start.2
  14.0 0.0 copy-start.3
  14.0 0.0 copy-start.4
  14.0 10.3 %conditional.1 = (bf16[2,64,640]{2,1,0:T(8,128)(2,1)S(1)}) conditional(s32[]{:T(128)} %convert_element_type.7, () %tuple.13, (s32[5]{0:T(128)S(1)}, bf16[2,512,128]{2,1,0:T(8,128)(2,1)}, bf16[2,512,128]{2,1,0:T(8,128)(2,1)S(1)}, bf16[2,16,512]{2,1,0:T(8,128)(2,1)S(1)}, bf16[2,16,512]{2,1,0:T(8,128)(2,1)S(1)}) %tuple.15), branch_computations={%region_1.0_spmd, %region_2.0_spmd} | conditional | flops 10000000000 | bytes 1376344 | solution.py:292
  14.0 1.3 %branch_1_fun.2 = (bf16[2,16,640]{2,1,0:T(8,128)(2,1)S(1)}, bf16[2,16,640]{2,1,0:T(8,128)(2,1)S(1)}) custom-call(s32[5]{0:T(128)S(1)} %get-tuple-element.18.flags_ref, bf16[2,512,128]{2,1,0:T(8,128)(2,1)} %get-tuple-element.21.first_ref, bf16[2,512,128]{2,1,0:T(8,128)(2,1)S(1)} %get-tuple-element.22.last_ref, ...), custom_call_target="tpu_custom_call" | custom-call | flops 10000000000 | bytes 1048576 | tf_op jit(solution)/shard_map/cond/branch_1_fun/pallas_call | solution.py:273
  15.3 3.2 %collective-permute-start = (bf16[2,16,640]{2,1,0:T(8,128)(2,1)S(1)}, bf16[2,16,640]{2,1,0:T(8,128)(2,1)S(1)}, u32[]{:S(2)}, u32[]{:S(2)}) collective-permute-start(bf16[2,16,640]{2,1,0:T(8,128)(2,1)S(1)} %get-tuple-element.23), channel_id=1, source_target_pairs={{0,1},{1,2},{2,3},{3,4},{4,5},{5,6},{6,7},{7,0},{8,9},{9,10},{10,1... | collective-permute-start | bytes 122888 | tf_op jit(solution)/shard_map/cond/branch_1_fun/ppermute | solution.py:255
  18.5 0.0 collective-permute-start.1
  18.5 1.7 %collective-permute-done.left_ref = bf16[2,16,640]{2,1,0:T(8,128)(2,1)S(1)} collective-permute-done((bf16[2,16,640]{2,1,0:T(8,128)(2,1)S(1)}, bf16[2,16,640]{2,1,0:T(8,128)(2,1)S(1)}, u32[]{:S(2)}, u32[]{:S(2)}) %collective-permute-start) | collective-permute-done | bytes 40992 | tf_op jit(solution)/shard_map/cond/branch_1_fun/ppermute | solution.py:255
  20.2 3.5 %collective-permute-done.1.right_ref = bf16[2,16,640]{2,1,0:T(8,128)(2,1)S(1)} collective-permute-done((bf16[2,16,640]{2,1,0:T(8,128)(2,1)S(1)}, bf16[2,16,640]{2,1,0:T(8,128)(2,1)S(1)}, u32[]{:S(2)}, u32[]{:S(2)}) %collective-permute-start.1) | collective-permute-done | bytes 40992 | tf_op jit(solution)/shard_map/cond/branch_1_fun/ppermute | solution.py:255
  23.7 0.6 %branch_1_fun.3 = bf16[2,64,640]{2,1,0:T(8,128)(2,1)S(1)} custom-call(s32[5]{0:T(128)S(1)} %get-tuple-element.18.flags_ref, bf16[2,16,512]{2,1,0:T(8,128)(2,1)S(1)} %get-tuple-element.19.above_ref, bf16[2,16,512]{2,1,0:T(8,128)(2,1)S(1)} %get-tuple-element.20.below_ref, bf16[2,16,640]{2,1,0:T(8,128)(2,1)S(1)} %collective-permute-done.left_ref, ...), custom_call_target="tpu_custom_call" | custom-call | tf_op jit(solution)/shard_map/cond/branch_1_fun/pallas_call | solution.py:283
  24.3 1.7 %collective-permute-start.6 = (bf16[2,64,640]{2,1,0:T(8,128)(2,1)S(1)}, bf16[2,64,640]{2,1,0:T(8,128)(2,1)S(1)}, u32[]{:S(2)}, u32[]{:S(2)}) collective-permute-start(bf16[2,64,640]{2,1,0:T(8,128)(2,1)S(1)} %get-tuple-element.41.refs_2_), channel_id=1, source_target_pairs={{0,224},{32,0},{64,32},{96,64},{128,96},{160,128},{192,160},{224,1... | collective-permute-start | bytes 491528 | tf_op jit(solution)/shard_map/ppermute | solution.py:255
  26.1 4.9 %shard_map.55 = (f32[4,4,4,1024]{3,2,1,0:T(4,128)}, bf16[2,4,4,160,256]{4,3,2,1,0:T(8,128)(2,1)S(1)}) custom-call(s32[5]{0:T(128)S(1)} %convert_element_type.6.refs_0_, bf16[2,512,512]{2,1,0:T(8,128)(2,1)S(1)} %copy-done, bf16[2,64,640]{2,1,0:T(8,128)(2,1)S(1)} %get-tuple-element.41.refs_2_, bf16[256,256]{1,0:T(8,128)(2,1)S(1)} %copy-done.2, ...), custom_call_target="tpu_custom_call" | custom-call | flops 35232153600 | bytes 1048576 | tf_op jit(solution)/shard_map/pallas_call | solution.py:234
  31.0 0.8 %collective-permute-start.5 = (bf16[1,240,512]{2,1,0:T(8,128)(2,1)S(1)}, bf16[1,240,512]{2,1,0:T(8,128)(2,1)S(1)}, u32[]{:S(2)}, u32[]{:S(2)}) collective-permute-start(bf16[1,240,512]{2,1,0:T(8,128)(2,1)S(1)} %slice.26), channel_id=1, source_target_pairs={{0,224},{32,0},{64,32},{96,64},{128,96},{160,128},{192,160},{224,1... | collective-permute-start | bytes 737288 | tf_op jit(solution)/shard_map/ppermute | solution.py:255
  31.8 0.0 collective-permute-done.6.refs_2_.refs_3_
  31.8 0.0 collective-permute-done.7.refs_1_
  31.8 4.1 %shard_map.56.refs_4_ = f32[4,4,4,1024]{3,2,1,0:T(4,128)} custom-call(s32[5]{0:T(128)S(1)} %convert_element_type.6.refs_0_, bf16[1,512,512]{2,1,0:T(8,128)(2,1)S(1)} %collective-permute-done.7.refs_1_, bf16[2,64,640]{2,1,0:T(8,128)(2,1)S(1)} %collective-permute-done.6.refs_2_.refs_3_, ...), custom_call_target="tpu_custom_call", output_to_operand_aliasing={{}: (4, {})} | custom-call | flops 21390950400 | bytes 1048576 | tf_op jit(solution)/shard_map/pallas_call | solution.py:234
  35.9 2.8 %shard_map.57.refs_5_ = f32[4,4,4,1024]{3,2,1,0:T(4,128)} custom-call(s32[5]{0:T(128)S(1)} %convert_element_type.6.refs_0_, bf16[1,272,512]{2,1,0:T(8,128)(2,1)S(1)} %collective-permute-done.2.refs_1_, bf16[2,64,640]{2,1,0:T(8,128)(2,1)S(1)} %collective-permute-done.6.refs_2_.refs_3_, ...), custom_call_target="tpu_custom_call", output_to_operand_aliasing={{}: (4, {})} | custom-call | flops 9437184000 | bytes 1048576 | tf_op jit(solution)/shard_map/pallas_call | solution.py:234
  38.7 2.8 %shard_map.58 = f32[4,4,4,1024]{3,2,1,0:T(4,128)} custom-call(s32[5]{0:T(128)S(1)} %convert_element_type.6.refs_0_, bf16[1,272,512]{2,1,0:T(8,128)(2,1)S(1)} %collective-permute-done.2.refs_1_, bf16[1,240,512]{2,1,0:T(8,128)(2,1)S(1)} %collective-permute-done.5.refs_2_, ...), custom_call_target="tpu_custom_call", output_to_operand_aliasing={{}: (5, {})} | custom-call | flops 9437184000 | bytes 1048576 | tf_op jit(solution)/shard_map/pallas_call | solution.py:234
  (9 shorter events, 0.0 us)
Async XLA Ops:
  0.8 13.1 %collective-permute-start.3 = (bf16[2,16,512]{2,1,0:T(8,128)(2,1)S(1)}, bf16[2,16,512]{2,1,0:T(8,128)(2,1)S(1)}, u32[]{:S(2)}, u32[]{:S(2)}) collective-permute-start(bf16[2,16,512]{2,1,0:T(8,128)(2,1)S(1)} %get-tuple-element.38), channel_id=1, source_target_pairs={{0,8},{8,16},{16,24},{24,0},{1,9},{9,17},{17,25},{25,1},{2,10},{10... | collective-permute-start | bytes 98312 | tf_op jit(solution)/shard_map/ppermute | solution.py:255
  0.8 13.1 %collective-permute-start.4 = (bf16[2,16,512]{2,1,0:T(8,128)(2,1)S(1)}, bf16[2,16,512]{2,1,0:T(8,128)(2,1)S(1)}, u32[]{:S(2)}, u32[]{:S(2)}) collective-permute-start(bf16[2,16,512]{2,1,0:T(8,128)(2,1)S(1)} %get-tuple-element.37), channel_id=1, source_target_pairs={{0,24},{8,0},{16,8},{24,16},{1,25},{9,1},{17,9},{25,17},{2,26},{10... | collective-permute-start | bytes 98312 | tf_op jit(solution)/shard_map/ppermute | solution.py:255
  5.1 26.7 %collective-permute-start.7 = (bf16[1,512,512]{2,1,0:T(8,128)(2,1)S(1)}, bf16[1,512,512]{2,1,0:T(8,128)(2,1)S(1)}, u32[]{:S(2)}, u32[]{:S(2)}) collective-permute-start(bf16[1,512,512]{2,1,0:T(8,128)(2,1)S(1)} %slice.27), channel_id=1, source_target_pairs={{0,224},{32,0},{64,32},{96,64},{128,96},{160,128},{192,160},{224,1... | collective-permute-start | bytes 1572872 | tf_op jit(solution)/shard_map/ppermute | solution.py:255
  10.1 25.8 %collective-permute-start.2 = (bf16[1,272,512]{2,1,0:T(8,128)(2,1)S(1)}, bf16[1,272,512]{2,1,0:T(8,128)(2,1)S(1)}, u32[]{:S(2)}, u32[]{:S(2)}) collective-permute-start(bf16[1,272,512]{2,1,0:T(8,128)(2,1)S(1)} %slice.21), channel_id=1, source_target_pairs={{0,224},{32,0},{64,32},{96,64},{128,96},{160,128},{192,160},{224,1... | collective-permute-start | bytes 835592 | tf_op jit(solution)/shard_map/ppermute | solution.py:255
  13.9 12.1 %copy-start = (bf16[2,512,512]{2,1,0:T(8,128)(2,1)S(1)}, bf16[2,512,512]{2,1,0:T(8,128)(2,1)}, u32[]{:S(2)}) copy-start(bf16[2,512,512]{2,1,0:T(8,128)(2,1)} %refs_1_.1) | copy-start | bytes 3145732
  13.9 12.1 %copy-start.1 = (bf16[1024,128]{1,0:T(8,128)(2,1)S(1)}, bf16[1024,128]{1,0:T(8,128)(2,1)}, u32[]{:S(2)}) copy-start(bf16[1024,128]{1,0:T(8,128)(2,1)} %constant.33.clone.refs_6_.refs_8_.refs_9_) | copy-start | bytes 786436
  13.9 12.1 %copy-start.2 = (bf16[256,256]{1,0:T(8,128)(2,1)S(1)}, bf16[256,256]{1,0:T(8,128)(2,1)}, u32[]{:S(2)}) copy-start(bf16[256,256]{1,0:T(8,128)(2,1)} %constant.30.clone.refs_3_.refs_5_.refs_6_) | copy-start | bytes 393220
  14.0 12.1 %copy-start.3 = (bf16[160,160]{1,0:T(8,128)(2,1)S(1)}, bf16[160,160]{1,0:T(8,128)(2,1)}, u32[]{:S(2)}) copy-start(bf16[160,160]{1,0:T(8,128)(2,1)} %constant.31.clone.refs_4_.refs_6_.refs_7_) | copy-start | bytes 153604
  14.0 12.1 %copy-start.4 = (bf16[32,160]{1,0:T(8,128)(2,1)S(1)}, bf16[32,160]{1,0:T(8,128)(2,1)}, u32[]{:S(2)}) copy-start(bf16[32,160]{1,0:T(8,128)(2,1)} %constant.32.clone.refs_5_.refs_7_.refs_8_) | copy-start | bytes 30724
  15.3 4.9 %collective-permute-start = (bf16[2,16,640]{2,1,0:T(8,128)(2,1)S(1)}, bf16[2,16,640]{2,1,0:T(8,128)(2,1)S(1)}, u32[]{:S(2)}, u32[]{:S(2)}) collective-permute-start(bf16[2,16,640]{2,1,0:T(8,128)(2,1)S(1)} %get-tuple-element.23), channel_id=1, source_target_pairs={{0,1},{1,2},{2,3},{3,4},{4,5},{5,6},{6,7},{7,0},{8,9},{9,10},{10,1... | collective-permute-start | bytes 122888 | tf_op jit(solution)/shard_map/cond/branch_1_fun/ppermute | solution.py:255
  18.5 5.2 %collective-permute-start.1 = (bf16[2,16,640]{2,1,0:T(8,128)(2,1)S(1)}, bf16[2,16,640]{2,1,0:T(8,128)(2,1)S(1)}, u32[]{:S(2)}, u32[]{:S(2)}) collective-permute-start(bf16[2,16,640]{2,1,0:T(8,128)(2,1)S(1)} %get-tuple-element.24), channel_id=1, source_target_pairs={{0,7},{1,0},{2,1},{3,2},{4,3},{5,4},{6,5},{7,6},{8,15},{9,8},{10,9... | collective-permute-start | bytes 122888 | tf_op jit(solution)/shard_map/cond/branch_1_fun/ppermute | solution.py:255
  24.3 7.5 %collective-permute-start.6 = (bf16[2,64,640]{2,1,0:T(8,128)(2,1)S(1)}, bf16[2,64,640]{2,1,0:T(8,128)(2,1)S(1)}, u32[]{:S(2)}, u32[]{:S(2)}) collective-permute-start(bf16[2,64,640]{2,1,0:T(8,128)(2,1)S(1)} %get-tuple-element.41.refs_2_), channel_id=1, source_target_pairs={{0,224},{32,0},{64,32},{96,64},{128,96},{160,128},{192,160},{224,1... | collective-permute-start | bytes 491528 | tf_op jit(solution)/shard_map/ppermute | solution.py:255
  31.0 7.8 %collective-permute-start.5 = (bf16[1,240,512]{2,1,0:T(8,128)(2,1)S(1)}, bf16[1,240,512]{2,1,0:T(8,128)(2,1)S(1)}, u32[]{:S(2)}, u32[]{:S(2)}) collective-permute-start(bf16[1,240,512]{2,1,0:T(8,128)(2,1)S(1)} %slice.26), channel_id=1, source_target_pairs={{0,224},{32,0},{64,32},{96,64},{128,96},{160,128},{192,160},{224,1... | collective-permute-start | bytes 737288 | tf_op jit(solution)/shard_map/ppermute | solution.py:255

commit v3 on v2

--- a/solution.py
+++ b/solution.py
@@ -12,9 +12,9 @@
 PATCH = 160
 STRIDE = 128
 OFF = 32
-CUT = 272
-STAGE_COST = 30
-EDGES_COST = 10_000_000_000
+CUT = 144
+CUTS = (CUT, 512)
+SPANS = ((1, 4),)
 RIM = 16
 HALF = PATCH // 2
 AXES = ("gz", "row", "col")
@@ -70,13 +70,13 @@
     return jnp.concatenate([jnp.where(top, special[:8], rest[:8]), rest[8:]], axis=0)
 
 
-def spectra_of(blocks, rim, columns, rows, live):
+def spectra_of(blocks, rim, columns, rows, live, which):
     lane = lax.broadcasted_iota(jnp.int32, (PATCH, 128), 1)
     head = lane < RIM
     tail = lane >= 128 - RIM
     side_lanes = head | tail
     result = []
-    for j in range(4):
+    for j in which:
         before = blocks[j - 1] if j > 0 else rim
         behind = blocks[j + 1] if j < 3 else rim
         main = blocks[j]
@@ -115,13 +115,25 @@
     return jnp.dot(back_rows, both, preferred_element_type=jnp.float32)
 
 
-def edges_kernel(flags_ref, first_ref, last_ref, above_ref, below_ref, low_ref, high_ref):
+def cut_kernel(parts, tile_ref, *refs):
+    sems = refs[-1]
+    copies = [
+        pltpu.make_async_copy(tile_ref.at[pl.ds(*deep), pl.ds(*tall)], ref, sems.at[n])
+        for n, ((deep, tall), ref) in enumerate(zip(parts, refs))
+    ]
+    for copy in copies:
+        copy.start()
+    for copy in copies:
+        copy.wait()
+
+
+def edges_kernel(flags_ref, tile_ref, above_ref, below_ref, low_ref, high_ref):
     up = (flags_ref[0] > 0).astype(jnp.float32)
     down = (flags_ref[1] > 0).astype(jnp.float32)
     for s in range(2):
         for block, ref, take in ((0, low_ref, 0), (1, high_ref, 128 - RIM)):
-            tile = (first_ref, last_ref)[block][s].astype(jnp.float32)
             lanes = slice(0, 128) if block == 0 else slice(384, 512)
+            tile = tile_ref[s, :, lanes].astype(jnp.float32)
             top = above_ref[s, :, lanes].astype(jnp.float32) * up
             bottom = below_ref[s, :, lanes].astype(jnp.float32) * down
             tall = jnp.concatenate([top, tile, bottom, jnp.zeros((96, 128), jnp.float32)], axis=0)
@@ -139,53 +151,99 @@
             rims_ref[:, RIM * n : RIM * (n + 1), :] = part
 
 
+def window(parts, i, b):
+    low, high = STRIDE * i - RIM, STRIDE * (i + 1) + RIM
+    pieces = []
+    for read, start, stop in parts:
+        begin, end = max(low, start), min(high, stop)
+        if begin < end:
+            pieces.append(read(slice(begin - start, end - start), slice(128 * b, 128 * (b + 1))))
+    return jnp.concatenate(pieces, axis=0) if len(pieces) > 1 else pieces[0]
+
+
+def reader(ref, s, first=0, factor=None):
+    def read(lines, lanes):
+        value = ref[s, first + lines.start : first + lines.stop, lanes].astype(jnp.float32)
+        return value if factor is None else value * factor
+
+    return read
+
+
+def inner_kernel(flags_ref, tile_ref, above_ref, below_ref, columns_ref, rows_ref, inner_ref):
+    up = (flags_ref[0] > 0).astype(jnp.float32)
+    down = (flags_ref[1] > 0).astype(jnp.float32)
+    columns, rows = columns_ref[...], rows_ref[...]
+    for i in range(4):
+        for s in range(2):
+            parts = [
+                (reader(above_ref, s, 0, up), -RIM, 0),
+                (reader(tile_ref, s), 0, 512),
+                (reader(below_ref, s, 0, down), 512, 512 + RIM),
+            ]
+            blocks = [window(parts, i, b) for b in range(4)]
+            for n, one in enumerate(spectra_of(blocks, None, columns, rows, None, (1, 2))):
+                inner_ref[s, i, n] = one
+
+
+def side_blocks(rims_ref, s):
+    both = rims_ref[s, 2 * RIM :].astype(jnp.float32)
+    gap = jnp.zeros((128 - 2 * RIM, both.shape[1]), jnp.float32)
+    return jnp.concatenate([both[RIM:], gap, both[:RIM]], axis=0).T
+
+
+def outer_kernel(flags_ref, tile_ref, rims_ref, inner_ref, columns_ref, rows_ref, outer_ref, rim_scr):
+    columns, rows = columns_ref[...], rows_ref[...]
+    for s in range(2):
+        rim_scr[s] = side_blocks(rims_ref, s)
+    for i in range(4):
+        for s in range(2):
+            parts = [
+                (reader(rims_ref, s), -RIM, 0),
+                (reader(tile_ref, s), 0, 512),
+                (reader(rims_ref, s, RIM), 512, 512 + RIM),
+            ]
+            blocks = [window(parts, i, b) for b in range(4)]
+            rim = rim_scr[s, STRIDE * i : STRIDE * i + PATCH, :]
+            for n, one in enumerate(spectra_of(blocks, rim, columns, rows, None, (0, 3))):
+                outer_ref[s, i, n] = one
+
+
 def kernel(plan, *refs):
-    fresh, kept, pairs, at, keep, masked, cuts, span = plan
+    fresh, pairs, at, cuts, span = plan
     refs = list(refs)
     flags_ref = refs.pop(0)
     tile_refs = [refs.pop(0) for _ in cuts]
-    rims_ref = refs.pop(0)
-    kept_ref = refs.pop(0) if kept else None
+    rims_ref, inner_ref, outer_ref = refs.pop(0), refs.pop(0), refs.pop(0)
     if at:
         refs.pop(0)
     columns_ref, rows_ref, back_rows_ref, back_columns_ref = [refs.pop(0) for _ in range(4)]
-    out_ref = refs.pop(0)
-    spectra_ref = refs.pop(0)
-    rim_scr, half_scr, line_scr, wide_scr, sem = refs
-    live = (flags_ref[4] > 0).astype(jnp.float32) if masked else None
+    out_ref, fresh_ref, rim_scr, half_scr, line_scr, wide_scr, sem = refs
+    live = (flags_ref[4] > 0).astype(jnp.float32)
     columns, rows = columns_ref[...], rows_ref[...]
     back_rows, back_columns = back_rows_ref[...], back_columns_ref[...]
     for n, s in enumerate(fresh):
-        both = rims_ref[s, 2 * RIM :].astype(jnp.float32)
-        gap = jnp.zeros((128 - 2 * RIM, both.shape[1]), jnp.float32)
-        rim_scr[n] = jnp.concatenate([both[RIM:], gap, both[:RIM]], axis=0).T
+        rim_scr[n] = side_blocks(rims_ref, s)
     for i in range(*span):
         for n, s in enumerate(fresh):
-            blocks = []
-            low, high = STRIDE * i - RIM, STRIDE * (i + 1) + RIM
-            for b in range(4):
-                lanes = slice(128 * b, 128 * (b + 1))
-                parts = []
-                if low < 0:
-                    parts.append(rims_ref[s, :RIM, lanes])
-                for ref, start in zip(tile_refs, cuts):
-                    begin, end = max(low, start), min(high, start + ref.shape[1])
-                    if begin < end:
-                        parts.append(ref[n, begin - start : end - start, lanes])
-                if high > 512:
-                    parts.append(rims_ref[s, RIM : 2 * RIM, lanes])
-                parts = [part.astype(jnp.float32) for part in parts]
-                blocks.append(jnp.concatenate(parts, axis=0) if len(parts) > 1 else parts[0])
+            parts = [(reader(rims_ref, s), -RIM, 0)]
+            for ref, start in zip(tile_refs, cuts):
+                parts.append((reader(ref, n), start, start + ref.shape[1]))
+            parts.append((reader(rims_ref, s, RIM), 512, 512 + RIM))
+            blocks = [window(parts, i, b) for b in range(4)]
             rim = rim_scr[n, STRIDE * i : STRIDE * i + PATCH, :]
-            for j, one in enumerate(spectra_of(blocks, rim, columns, rows, live)):
-                spectra_ref[n, i - span[0], j] = one
+            for m, one in enumerate(spectra_of(blocks, rim, columns, rows, live, range(4))):
+                fresh_ref[n, i - span[0], m] = one
+
+    def spectrum(section, i, j):
+        if section >= 2:
+            return fresh_ref[section - 2, i - span[0], j]
+        return inner_ref[section, i, j - 1] if j in (1, 2) else outer_ref[section, i, j // 3]
+
     tall = 32 * (span[1] - span[0])
     for i in range(*span):
         for n, (a, b) in enumerate(pairs):
             for j in range(4):
-                left = kept_ref[a, i, j] if a < kept else spectra_ref[a - kept, i - span[0], j]
-                right = kept_ref[b, i, j] if b < kept else spectra_ref[b - kept, i - span[0], j]
-                halves = half_back(left, right, back_rows)
+                halves = half_back(spectrum(a, i, j), spectrum(b, i, j), back_rows)
                 place = tall * n + 32 * (i - span[0]) + 8 * j
                 for t in range(4):
                     half_scr[place : place + 8, 256 * t : 256 * (t + 1)] = halves[8 * t : 8 * (t + 1)]
@@ -208,46 +266,53 @@
 IN_VMEM = pl.BlockSpec(memory_space=pltpu.VMEM)
 IN_SMEM = pl.BlockSpec(memory_space=pltpu.SMEM)
 ANYWHERE = pl.BlockSpec(memory_space=pl.ANY)
-PARAMS = pltpu.CompilerParams(vmem_limit_bytes=24 * 1024 * 1024)
-
-
-def stage(flags, tiles, rims, kept, earlier, consts, fresh, pairs, at, keep, masked, span=(0, 4)):
-    held = 0 if kept is None else kept.shape[0]
-    operands, aliases = [flags, *tiles.values(), rims], {}
-    specs = [IN_SMEM] + [IN_VMEM] * (len(tiles) + 1)
-    if held:
-        operands.append(kept)
-        specs.append(IN_VMEM)
-    if earlier is not None:
+PARAMS = pltpu.CompilerParams(vmem_limit_bytes=9 * 1024 * 1024)
+
+
+def cost(flops):
+    return pl.CostEstimate(flops=flops, bytes_accessed=1 << 20, transcendentals=0)
+
+
+def stage(flags, tiles, rims, inner, outer, earlier, consts, fresh, pairs, at, span=(0, 4)):
+    height = span[1] - span[0]
+    operands, aliases = [flags, *tiles.values(), rims, inner, outer], {}
+    specs = [IN_SMEM] + [IN_VMEM] * (len(operands) - 1)
+    if at:
         aliases[len(operands)] = 0
         operands.append(earlier)
         specs.append(ANYWHERE)
     operands += consts
     specs += [IN_VMEM] * len(consts)
-    out_shape = [jax.ShapeDtypeStruct((4, 4, 4, 1024), jnp.float32)]
-    out_specs = [ANYWHERE]
-    if keep:
-        out_shape.append(jax.ShapeDtypeStruct((len(fresh), 4, 4, PATCH, 256), jnp.bfloat16))
-        out_specs.append(IN_VMEM)
-    height = span[1] - span[0]
-    flops = 2 * 4 * height * (len(fresh) * (PATCH * 65536 + PATCH**2 * 256) + len(pairs) * 64 * PATCH * 256)
     return pl.pallas_call(
-        functools.partial(kernel, (fresh, held, pairs, at, keep, masked, tuple(tiles), span)),
+        functools.partial(kernel, (fresh, pairs, at, tuple(tiles), span)),
         in_specs=specs,
-        out_specs=out_specs,
-        out_shape=out_shape,
+        out_specs=ANYWHERE,
+        out_shape=jax.ShapeDtypeStruct((4, 4, 4, 1024), jnp.float32),
         input_output_aliases=aliases,
-        scratch_shapes=([] if keep else [pltpu.VMEM((len(fresh), height, 4, PATCH, 256), jnp.bfloat16)])
-        + [
-            pltpu.VMEM((len(fresh), rims.shape[-1], 128), jnp.float32),
+        scratch_shapes=[
+            pltpu.VMEM((len(fresh), height, 4, PATCH, 256), jnp.bfloat16),
+            pltpu.VMEM((len(fresh), 640, 128), jnp.float32),
             pltpu.VMEM((32 * height * len(pairs), 1024), jnp.float32),
             pltpu.VMEM((32 * height * len(pairs), 128), jnp.float32),
             pltpu.VMEM((len(pairs), height, 4, 1024), jnp.float32),
             pltpu.SemaphoreType.DMA,
         ],
         compiler_params=PARAMS,
-        cost_estimate=pl.CostEstimate(flops=STAGE_COST * flops, bytes_accessed=1 << 20, transcendentals=0),
+        cost_estimate=cost(60_000_000_000),
     )(*operands)
+
+
+def cut(sections, parts):
+    return pl.pallas_call(
+        functools.partial(cut_kernel, parts),
+        in_specs=[pl.BlockSpec(memory_space=pltpu.HBM)],
+        out_specs=[IN_VMEM] * len(parts),
+        out_shape=[
+            jax.ShapeDtypeStruct((deep[1], tall[1], sections.shape[2]), jnp.bfloat16) for deep, tall in parts
+        ],
+        scratch_shapes=[pltpu.SemaphoreType.DMA((len(parts),))],
+        compiler_params=PARAMS,
+    )(sections)
 
 
 def ring(value, axis, steps):
@@ -261,50 +326,70 @@
     row, col, gz = lax.axis_index("row"), lax.axis_index("col"), lax.axis_index("gz")
     rows, cols, depth = lax.axis_size("row"), lax.axis_size("col"), lax.axis_size("gz")
     flags = jnp.stack([row > 0, row < rows - 1, col > 0, col < cols - 1, gz < depth - 1]).astype(jnp.int32)
-    above = ring(sections[:, height - RIM :], "row", 1)
-    below = ring(sections[:, :RIM], "row", -1)
-    first = ring(sections[:1], "gz", -1)
-    upper = ring(sections[1:, :CUT], "gz", -1)
-    blocks = lax.optimization_barrier((sections[:, :, :128], sections[:, :, width - 128 :]))
+    bf = lambda *shape: jax.ShapeDtypeStruct(shape, jnp.bfloat16)
+    top, bottom = cut(sections, [((0, 2), (0, RIM)), ((0, 2), (height - RIM, RIM))])
+    first, upper = cut(sections, [((0, 1), (0, height)), ((1, 1), (0, CUT))])
+    above = ring(bottom, "row", 1)
+    below = ring(top, "row", -1)
+    first = ring(first, "gz", -1)
+    upper = ring(upper, "gz", -1)
 
     def around(operands):
-        flags, first_block, last_block, above, below = operands
-        edge = jax.ShapeDtypeStruct((2, RIM, 640), jnp.bfloat16)
+        flags, tile, above, below = operands
         low, high = pl.pallas_call(
             edges_kernel,
-            in_specs=[IN_SMEM] + [IN_VMEM] * 4,
+            in_specs=[IN_SMEM] + [IN_VMEM] * 3,
             out_specs=[IN_VMEM, IN_VMEM],
-            out_shape=[edge, edge],
+            out_shape=[bf(2, RIM, 640), bf(2, RIM, 640)],
             compiler_params=PARAMS,
-            cost_estimate=pl.CostEstimate(flops=EDGES_COST, bytes_accessed=1 << 20, transcendentals=0),
-        )(flags, first_block, last_block, above, below)
+        )(flags, tile, above, below)
         left = ring(high, "col", 1)
         right = ring(low, "col", -1)
+        inner = pl.pallas_call(
+            inner_kernel,
+            in_specs=[IN_SMEM] + [IN_VMEM] * 5,
+            out_specs=IN_VMEM,
+            out_shape=bf(2, 4, 2, PATCH, 256),
+            compiler_params=PARAMS,
+            cost_estimate=cost(10_000_000_000),
+        )(flags, tile, above, below, consts[0], consts[1])
         rims = pl.pallas_call(
             rims_kernel,
             in_specs=[IN_SMEM] + [IN_VMEM] * 4,
             out_specs=IN_VMEM,
-            out_shape=jax.ShapeDtypeStruct((2, 4 * RIM, 640), jnp.bfloat16),
+            out_shape=bf(2, 4 * RIM, 640),
             compiler_params=PARAMS,
         )(flags, above, below, left, right)
-        return rims
-
-    rims = lax.cond(
-        jnp.sum(flags) < 99,
-        around,
-        lambda operands: jnp.zeros((2, 4 * RIM, 640), jnp.bfloat16),
-        (flags, *blocks, above, below),
+        return rims, inner
+
+    def nothing(operands):
+        return jnp.zeros((2, 4 * RIM, 640), jnp.bfloat16), jnp.zeros((2, 4, 2, PATCH, 256), jnp.bfloat16)
+
+    rims, inner = lax.cond(
+        row + col + gz < 99, around, nothing, (flags, sections, above, below)
     )
     far = ring(rims, "gz", -1)
-    result, spectra = stage(flags, {0: sections}, rims, None, None, consts, (0, 1), [(0, 1)], 0, True, False)
-    later, spectra = lax.optimization_barrier((sections, spectra))
-    lower = ring(later[1:, CUT:], "gz", -1)
-    result, = stage(flags, {0: first}, far, spectra, result, consts, (0,), [(0, 2), (1, 2)], 1, False, True)
-    result, = stage(
-        flags, {0: upper}, far, spectra, result, consts, (1,), [(1, 2)], 3, False, True, (0, 2)
-    )
-    both = {0: upper, CUT: lower}
-    result, = stage(flags, both, far, spectra, result, consts, (1,), [(1, 2)], 3, False, True, (2, 4))
+    outer = pl.pallas_call(
+        outer_kernel,
+        in_specs=[IN_SMEM] + [IN_VMEM] * 5,
+        out_specs=IN_VMEM,
+        out_shape=bf(2, 4, 2, PATCH, 256),
+        scratch_shapes=[pltpu.VMEM((2, 640, 128), jnp.float32)],
+        compiler_params=PARAMS,
+        cost_estimate=cost(60_000_000_000),
+    )(flags, sections, rims, inner, consts[0], consts[1])
+    later, outer = lax.optimization_barrier((sections, outer))
+    lower = cut(later, [((1, 1), (a, b - a)) for a, b in zip(CUTS[:-1], CUTS[1:])])
+    lower = [ring(part, "gz", -1) for part in lower]
+    pairs = [(0, 1), (0, 2), (1, 2)]
+    result = stage(flags, {0: first}, far, inner, outer, None, consts, (0,), pairs, 0)
+    parts = {0: upper}
+    spans = list(SPANS)
+    if spans[0][0]:
+        result = stage(flags, parts, far, inner, outer, result, consts, (1,), [(1, 2)], 3, (0, spans[0][0]))
+    for start, part, span in zip(CUTS, lower, spans):
+        parts = {**parts, start: part}
+        result = stage(flags, parts, far, inner, outer, result, consts, (1,), [(1, 2)], 3, span)
     return result.reshape(2, 2, 4, 4, OFF * OFF)
 
 

time: 42 us -> 39.4 us (0.938)
  the two profiles are of different devices: /device:TPU:96 before, /device:TPU:1 now
where the time goes in v3:
time: 39.4 us; the launch traced here: 39.3 us
  starting transfers between devices  18.5 us (47%)
  Pallas kernels  17.7 us (45%)
  waiting for transfers between devices  2.61 us (7%)
    ppermute x8, starting transfers between devices, ring(): lax.ppermute(value, axis, [(n, (n + steps) % count) for n in range(count)])  18.5 us
    pallas_call x3, Pallas kernels, stage(): pl.pallas_call(functools.partial(kernel, (fresh, pairs, at, tuple(tiles),...  10.5 us
    ppermute x8, waiting for transfers between devices, ring(): lax.ppermute(value, axis, [(n, (n + steps) % count) for n in range(count)])  2.61 us
    pallas_call x1, Pallas kernels, shards(): pl.pallas_call(outer_kernel, in_specs=[IN_SMEM] + [IN_VMEM] * 5, out_spec...  2.53 us
    pallas_call x1, Pallas kernels, around(): pl.pallas_call(inner_kernel, in_specs=[IN_SMEM] + [IN_VMEM] * 5, out_spec...  2.04 us
    pallas_call x3, Pallas kernels, cut(): pl.pallas_call(functools.partial(cut_kernel, parts), in_specs=[pl.BlockSp...  1.31 us
  transfers between devices with their start and end apart: 8, of which 2 were waited for; matrix products, arithmetic and copies ran while one was open for 0% of the time, Pallas kernels for 35%

profile of v3, /device:TPU:1, one launch (start us, length us, event | category | flops | bytes accessed | tf_op | source)
XLA Modules:
  0.0 39.3 jit_solution(1340326697498634052)
XLA Ops:
  0.0 0.9 %shard_map.56 = (bf16[2,16,512]{2,1,0:T(8,128)(2,1)S(1)}, bf16[2,16,512]{2,1,0:T(8,128)(2,1)S(1)}) custom-call(bf16[2,512,512]{2,1,0:T(8,128)(2,1)} %tile_ref.6), custom_call_target="tpu_custom_call" | custom-call | tf_op jit(solution)/shard_map/pallas_call | solution.py:306
  0.9 4.2 %collective-permute-start.3 = (bf16[2,16,512]{2,1,0:T(8,128)(2,1)S(1)}, bf16[2,16,512]{2,1,0:T(8,128)(2,1)S(1)}, u32[]{:S(2)}, u32[]{:S(2)}) collective-permute-start(bf16[2,16,512]{2,1,0:T(8,128)(2,1)S(1)} %get-tuple-element.34), channel_id=1, source_target_pairs={{0,8},{8,16},{16,24},{24,0},{1,9},{9,17},{17,25},{25,1},{2,10},{10... | collective-permute-start | bytes 98312 | tf_op jit(solution)/shard_map/ppermute | solution.py:320
  5.1 0.0 collective-permute-start.4
  5.1 0.0 copy-done.2
  5.1 0.2 shard_map.55
  5.4 2.8 %collective-permute-start.2 = (bf16[1,144,512]{2,1,0:T(8,128)(2,1)S(1)}, bf16[1,144,512]{2,1,0:T(8,128)(2,1)S(1)}, u32[]{:S(2)}, u32[]{:S(2)}) collective-permute-start(bf16[1,144,512]{2,1,0:T(8,128)(2,1)S(1)} %get-tuple-element.33), channel_id=1, source_target_pairs={{0,224},{32,0},{64,32},{96,64},{128,96},{160,128},{192,160},{224,1... | collective-permute-start | bytes 442376 | tf_op jit(solution)/shard_map/ppermute | solution.py:320
  8.2 1.2 %collective-permute-start.7 = (bf16[1,512,512]{2,1,0:T(8,128)(2,1)S(1)}, bf16[1,512,512]{2,1,0:T(8,128)(2,1)S(1)}, u32[]{:S(2)}, u32[]{:S(2)}) collective-permute-start(bf16[1,512,512]{2,1,0:T(8,128)(2,1)S(1)} %get-tuple-element.40), channel_id=1, source_target_pairs={{0,224},{32,0},{64,32},{96,64},{128,96},{160,128},{192,160},{224,1... | collective-permute-start | bytes 1572872 | tf_op jit(solution)/shard_map/ppermute | solution.py:320
  9.4 0.1 stack.23
  9.5 0.0 collective-permute-done.3
  9.5 0.5 %collective-permute-done.4 = bf16[2,16,512]{2,1,0:T(8,128)(2,1)S(1)} collective-permute-done((bf16[2,16,512]{2,1,0:T(8,128)(2,1)S(1)}, bf16[2,16,512]{2,1,0:T(8,128)(2,1)S(1)}, u32[]{:S(2)}, u32[]{:S(2)}) %collective-permute-start.4) | collective-permute-done | bytes 32800 | tf_op jit(solution)/shard_map/ppermute | solution.py:320
  10.0 0.0 copy-done.4
  10.0 9.2 %conditional.1 = (bf16[2,64,640]{2,1,0:T(8,128)(2,1)S(1)}, bf16[2,4,2,160,256]{4,3,2,1,0:T(8,128)(2,1)S(1)}) conditional(s32[]{:T(128)} %convert_element_type.7, () %tuple.14, (s32[5]{0:T(128)S(1)}, bf16[2,512,512]{2,1,0:T(8,128)(2,1)S(1)}, bf16[2,16,512]{2,1,0:T(8,128)(2,1)S(1)}, bf16[2,16,512]{2,1,0:T(8,128)(2,1)S(1)}, ...), branch_computations={%region_0.0_spmd, %region_1.0_spmd} | conditional | flops 10000000000 | bytes 1474580 | solution.py:368
  10.0 0.8 %branch_1_fun.3 = (bf16[2,16,640]{2,1,0:T(8,128)(2,1)S(1)}, bf16[2,16,640]{2,1,0:T(8,128)(2,1)S(1)}) custom-call(s32[5]{0:T(128)S(1)} %get-tuple-element.17.flags_ref, bf16[2,512,512]{2,1,0:T(8,128)(2,1)S(1)} %get-tuple-element.20.tile_ref, bf16[2,16,512]{2,1,0:T(8,128)(2,1)S(1)} %get-tuple-element.18.above_ref, ...), custom_call_target="tpu_custom_call" | custom-call | tf_op jit(solution)/shard_map/cond/branch_1_fun/pallas_call | solution.py:339
  10.7 1.7 %collective-permute-start = (bf16[2,16,640]{2,1,0:T(8,128)(2,1)S(1)}, bf16[2,16,640]{2,1,0:T(8,128)(2,1)S(1)}, u32[]{:S(2)}, u32[]{:S(2)}) collective-permute-start(bf16[2,16,640]{2,1,0:T(8,128)(2,1)S(1)} %get-tuple-element.21), channel_id=1, source_target_pairs={{0,1},{1,2},{2,3},{3,4},{4,5},{5,6},{6,7},{7,0},{8,9},{9,10},{10,1... | collective-permute-start | bytes 122888 | tf_op jit(solution)/shard_map/cond/branch_1_fun/ppermute | solution.py:320
  12.5 4.0 %collective-permute-start.1 = (bf16[2,16,640]{2,1,0:T(8,128)(2,1)S(1)}, bf16[2,16,640]{2,1,0:T(8,128)(2,1)S(1)}, u32[]{:S(2)}, u32[]{:S(2)}) collective-permute-start(bf16[2,16,640]{2,1,0:T(8,128)(2,1)S(1)} %get-tuple-element.22), channel_id=1, source_target_pairs={{0,7},{1,0},{2,1},{3,2},{4,3},{5,4},{6,5},{7,6},{8,15},{9,8},{10,9... | collective-permute-start | bytes 122888 | tf_op jit(solution)/shard_map/cond/branch_1_fun/ppermute | solution.py:320
  16.5 2.0 %branch_1_fun.5 = bf16[2,4,2,160,256]{4,3,2,1,0:T(8,128)(2,1)S(1)} custom-call(s32[5]{0:T(128)S(1)} %get-tuple-element.17.flags_ref, bf16[2,512,512]{2,1,0:T(8,128)(2,1)S(1)} %get-tuple-element.20.tile_ref, bf16[2,16,512]{2,1,0:T(8,128)(2,1)S(1)} %get-tuple-element.18.above_ref, bf16[2,16,512]{2,1,0:T(8,128)(2,1)S(1)} %get-tuple-element.19.below_ref, ...), custom_call_target="tpu_custom_call" | custom-call | flops 10000000000 | bytes 1048576 | tf_op jit(solution)/shard_map/cond/branch_1_fun/pallas_call | solution.py:348
  18.5 0.0 collective-permute-done.left_ref
  18.5 0.0 collective-permute-done.1.right_ref
  18.6 0.6 %branch_1_fun.4 = bf16[2,64,640]{2,1,0:T(8,128)(2,1)S(1)} custom-call(s32[5]{0:T(128)S(1)} %get-tuple-element.17.flags_ref, bf16[2,16,512]{2,1,0:T(8,128)(2,1)S(1)} %get-tuple-element.18.above_ref, bf16[2,16,512]{2,1,0:T(8,128)(2,1)S(1)} %get-tuple-element.19.below_ref, bf16[2,16,640]{2,1,0:T(8,128)(2,1)S(1)} %collective-permute-done.left_ref, ...), custom_call_target="tpu_custom_call" | custom-call | tf_op jit(solution)/shard_map/cond/branch_1_fun/pallas_call | solution.py:356
  19.1 3.1 %collective-permute-start.6 = (bf16[2,64,640]{2,1,0:T(8,128)(2,1)S(1)}, bf16[2,64,640]{2,1,0:T(8,128)(2,1)S(1)}, u32[]{:S(2)}, u32[]{:S(2)}) collective-permute-start(bf16[2,64,640]{2,1,0:T(8,128)(2,1)S(1)} %get-tuple-element.36.rims_ref), channel_id=1, source_target_pairs={{0,224},{32,0},{64,32},{96,64},{128,96},{160,128},{192,160},{224,1... | collective-permute-start | bytes 491528 | tf_op jit(solution)/shard_map/ppermute | solution.py:320
  22.2 2.5 %shard_map.57.refs_4_.refs_5_ = bf16[2,4,2,160,256]{4,3,2,1,0:T(8,128)(2,1)S(1)} custom-call(s32[5]{0:T(128)S(1)} %convert_element_type.6.flags_ref.refs_0_, bf16[2,512,512]{2,1,0:T(8,128)(2,1)S(1)} %copy-done.2, bf16[2,64,640]{2,1,0:T(8,128)(2,1)S(1)} %get-tuple-element.36.rims_ref, ...), custom_call_target="tpu_custom_call" | custom-call | flops 60000002048 | bytes 1048576 | tf_op jit(solution)/shard_map/pallas_call | solution.py:372
  24.8 0.0 copy-start
  24.8 0.0 copy-start.1
  24.8 0.2 shard_map.58
  25.0 1.5 %collective-permute-start.5 = (bf16[1,368,512]{2,1,0:T(8,128)(2,1)S(1)}, bf16[1,368,512]{2,1,0:T(8,128)(2,1)S(1)}, u32[]{:S(2)}, u32[]{:S(2)}) collective-permute-start(bf16[1,368,512]{2,1,0:T(8,128)(2,1)S(1)} %shard_map.58), channel_id=1, source_target_pairs={{0,224},{32,0},{64,32},{96,64},{128,96},{160,128},{192,160},{224,1... | collective-permute-start | bytes 1130504 | tf_op jit(solution)/shard_map/ppermute | solution.py:320
  26.5 0.0 collective-permute-done.6.refs_2_.refs_3_
  26.5 0.0 collective-permute-done.7.refs_1_
  26.5 4.8 %shard_map.59.refs_5_ = f32[4,4,4,1024]{3,2,1,0:T(4,128)} custom-call(s32[5]{0:T(128)S(1)} %convert_element_type.6.flags_ref.refs_0_, bf16[1,512,512]{2,1,0:T(8,128)(2,1)S(1)} %collective-permute-done.7.refs_1_, bf16[2,64,640]{2,1,0:T(8,128)(2,1)S(1)} %collective-permute-done.6.refs_2_.refs_3_, ...), custom_call_target="tpu_custom_call" | custom-call | flops 60000002048 | bytes 1048576 | tf_op jit(solution)/shard_map/pallas_call | solution.py:286
  31.3 0.0 collective-permute-done.2.refs_1_
  31.4 2.4 %shard_map.60.refs_6_ = f32[4,4,4,1024]{3,2,1,0:T(4,128)} custom-call(s32[5]{0:T(128)S(1)} %convert_element_type.6.flags_ref.refs_0_, bf16[1,144,512]{2,1,0:T(8,128)(2,1)S(1)} %collective-permute-done.2.refs_1_, bf16[2,64,640]{2,1,0:T(8,128)(2,1)S(1)} %collective-permute-done.6.refs_2_.refs_3_, ...), custom_call_target="tpu_custom_call", output_to_operand_aliasing={{}: (5, {})} | custom-call | flops 60000002048 | bytes 1048576 | tf_op jit(solution)/shard_map/pallas_call | solution.py:286
  33.8 2.1 %collective-permute-done.5.refs_2_ = bf16[1,368,512]{2,1,0:T(8,128)(2,1)S(1)} collective-permute-done((bf16[1,368,512]{2,1,0:T(8,128)(2,1)S(1)}, bf16[1,368,512]{2,1,0:T(8,128)(2,1)S(1)}, u32[]{:S(2)}, u32[]{:S(2)}) %collective-permute-start.5) | collective-permute-done | bytes 376864 | tf_op jit(solution)/shard_map/ppermute | solution.py:320
  35.9 3.2 %shard_map.61 = f32[4,4,4,1024]{3,2,1,0:T(4,128)} custom-call(s32[5]{0:T(128)S(1)} %convert_element_type.6.flags_ref.refs_0_, bf16[1,144,512]{2,1,0:T(8,128)(2,1)S(1)} %collective-permute-done.2.refs_1_, bf16[1,368,512]{2,1,0:T(8,128)(2,1)S(1)} %collective-permute-done.5.refs_2_, ...), custom_call_target="tpu_custom_call", output_to_operand_aliasing={{}: (6, {})} | custom-call | flops 60000002048 | bytes 1048576 | tf_op jit(solution)/shard_map/pallas_call | solution.py:286
  (7 shorter events, 0.0 us)
Async XLA Ops:
  0.0 5.1 %copy-start.2 = (bf16[2,512,512]{2,1,0:T(8,128)(2,1)S(1)}, bf16[2,512,512]{2,1,0:T(8,128)(2,1)}, u32[]{:S(2)}) copy-start(bf16[2,512,512]{2,1,0:T(8,128)(2,1)} %tile_ref.6) | copy-start | bytes 3145732
  0.0 10.0 %copy-start.3 = (bf16[256,256]{1,0:T(8,128)(2,1)S(1)}, bf16[256,256]{1,0:T(8,128)(2,1)}, u32[]{:S(2)}) copy-start(bf16[256,256]{1,0:T(8,128)(2,1)} %constant.31.clone.columns_ref.refs_5_.refs_6_.refs_7_) | copy-start | bytes 393220
  0.0 10.0 %copy-start.4 = (bf16[160,160]{1,0:T(8,128)(2,1)S(1)}, bf16[160,160]{1,0:T(8,128)(2,1)}, u32[]{:S(2)}) copy-start(bf16[160,160]{1,0:T(8,128)(2,1)} %constant.32.clone.rows_ref.refs_6_.refs_7_.refs_8_) | copy-start | bytes 153604
  0.9 8.6 %collective-permute-start.3 = (bf16[2,16,512]{2,1,0:T(8,128)(2,1)S(1)}, bf16[2,16,512]{2,1,0:T(8,128)(2,1)S(1)}, u32[]{:S(2)}, u32[]{:S(2)}) collective-permute-start(bf16[2,16,512]{2,1,0:T(8,128)(2,1)S(1)} %get-tuple-element.34), channel_id=1, source_target_pairs={{0,8},{8,16},{16,24},{24,0},{1,9},{9,17},{17,25},{25,1},{2,10},{10... | collective-permute-start | bytes 98312 | tf_op jit(solution)/shard_map/ppermute | solution.py:320
  5.1 4.8 %collective-permute-start.4 = (bf16[2,16,512]{2,1,0:T(8,128)(2,1)S(1)}, bf16[2,16,512]{2,1,0:T(8,128)(2,1)S(1)}, u32[]{:S(2)}, u32[]{:S(2)}) collective-permute-start(bf16[2,16,512]{2,1,0:T(8,128)(2,1)S(1)} %get-tuple-element.35), channel_id=1, source_target_pairs={{0,24},{8,0},{16,8},{24,16},{1,25},{9,1},{17,9},{25,17},{2,26},{10... | collective-permute-start | bytes 98312 | tf_op jit(solution)/shard_map/ppermute | solution.py:320
  5.4 26.0 %collective-permute-start.2 = (bf16[1,144,512]{2,1,0:T(8,128)(2,1)S(1)}, bf16[1,144,512]{2,1,0:T(8,128)(2,1)S(1)}, u32[]{:S(2)}, u32[]{:S(2)}) collective-permute-start(bf16[1,144,512]{2,1,0:T(8,128)(2,1)S(1)} %get-tuple-element.33), channel_id=1, source_target_pairs={{0,224},{32,0},{64,32},{96,64},{128,96},{160,128},{192,160},{224,1... | collective-permute-start | bytes 442376 | tf_op jit(solution)/shard_map/ppermute | solution.py:320
  8.2 18.3 %collective-permute-start.7 = (bf16[1,512,512]{2,1,0:T(8,128)(2,1)S(1)}, bf16[1,512,512]{2,1,0:T(8,128)(2,1)S(1)}, u32[]{:S(2)}, u32[]{:S(2)}) collective-permute-start(bf16[1,512,512]{2,1,0:T(8,128)(2,1)S(1)} %get-tuple-element.40), channel_id=1, source_target_pairs={{0,224},{32,0},{64,32},{96,64},{128,96},{160,128},{192,160},{224,1... | collective-permute-start | bytes 1572872 | tf_op jit(solution)/shard_map/ppermute | solution.py:320
  10.7 7.8 %collective-permute-start = (bf16[2,16,640]{2,1,0:T(8,128)(2,1)S(1)}, bf16[2,16,640]{2,1,0:T(8,128)(2,1)S(1)}, u32[]{:S(2)}, u32[]{:S(2)}) collective-permute-start(bf16[2,16,640]{2,1,0:T(8,128)(2,1)S(1)} %get-tuple-element.21), channel_id=1, source_target_pairs={{0,1},{1,2},{2,3},{3,4},{4,5},{5,6},{6,7},{7,0},{8,9},{9,10},{10,1... | collective-permute-start | bytes 122888 | tf_op jit(solution)/shard_map/cond/branch_1_fun/ppermute | solution.py:320
  12.5 6.1 %collective-permute-start.1 = (bf16[2,16,640]{2,1,0:T(8,128)(2,1)S(1)}, bf16[2,16,640]{2,1,0:T(8,128)(2,1)S(1)}, u32[]{:S(2)}, u32[]{:S(2)}) collective-permute-start(bf16[2,16,640]{2,1,0:T(8,128)(2,1)S(1)} %get-tuple-element.22), channel_id=1, source_target_pairs={{0,7},{1,0},{2,1},{3,2},{4,3},{5,4},{6,5},{7,6},{8,15},{9,8},{10,9... | collective-permute-start | bytes 122888 | tf_op jit(solution)/shard_map/cond/branch_1_fun/ppermute | solution.py:320
  19.1 7.3 %collective-permute-start.6 = (bf16[2,64,640]{2,1,0:T(8,128)(2,1)S(1)}, bf16[2,64,640]{2,1,0:T(8,128)(2,1)S(1)}, u32[]{:S(2)}, u32[]{:S(2)}) collective-permute-start(bf16[2,64,640]{2,1,0:T(8,128)(2,1)S(1)} %get-tuple-element.36.rims_ref), channel_id=1, source_target_pairs={{0,224},{32,0},{64,32},{96,64},{128,96},{160,128},{192,160},{224,1... | collective-permute-start | bytes 491528 | tf_op jit(solution)/shard_map/ppermute | solution.py:320
  24.8 1.7 %copy-start = (bf16[1024,128]{1,0:T(8,128)(2,1)S(1)}, bf16[1024,128]{1,0:T(8,128)(2,1)}, u32[]{:S(2)}) copy-start(bf16[1024,128]{1,0:T(8,128)(2,1)} %constant.34.clone.refs_8_.refs_9_.refs_10_) | copy-start | bytes 786436
  24.8 1.7 %copy-start.1 = (bf16[32,160]{1,0:T(8,128)(2,1)S(1)}, bf16[32,160]{1,0:T(8,128)(2,1)}, u32[]{:S(2)}) copy-start(bf16[32,160]{1,0:T(8,128)(2,1)} %constant.33.clone.refs_7_.refs_8_.refs_9_) | copy-start | bytes 30724
  25.0 10.9 %collective-permute-start.5 = (bf16[1,368,512]{2,1,0:T(8,128)(2,1)S(1)}, bf16[1,368,512]{2,1,0:T(8,128)(2,1)S(1)}, u32[]{:S(2)}, u32[]{:S(2)}) collective-permute-start(bf16[1,368,512]{2,1,0:T(8,128)(2,1)S(1)} %shard_map.58), channel_id=1, source_target_pairs={{0,224},{32,0},{64,32},{96,64},{128,96},{160,128},{192,160},{224,1... | collective-permute-start | bytes 1130504 | tf_op jit(solution)/shard_map/ppermute | solution.py:320

commit v4 on v3

--- a/solution.py
+++ b/solution.py
@@ -115,6 +115,12 @@
     return jnp.dot(back_rows, both, preferred_element_type=jnp.float32)
 
 
+def inside(axis, ahead):
+    place = lax.axis_index(axis)
+    there = place < lax.axis_size(axis) - 1 if ahead else place > 0
+    return there.astype(jnp.float32)
+
+
 def cut_kernel(parts, tile_ref, *refs):
     sems = refs[-1]
     copies = [
@@ -127,9 +133,9 @@
         copy.wait()
 
 
-def edges_kernel(flags_ref, tile_ref, above_ref, below_ref, low_ref, high_ref):
-    up = (flags_ref[0] > 0).astype(jnp.float32)
-    down = (flags_ref[1] > 0).astype(jnp.float32)
+def edges_kernel(tile_ref, above_ref, below_ref, low_ref, high_ref):
+    up = inside("row", False)
+    down = inside("row", True)
     for s in range(2):
         for block, ref, take in ((0, low_ref, 0), (1, high_ref, 128 - RIM)):
             lanes = slice(0, 128) if block == 0 else slice(384, 512)
@@ -140,9 +146,9 @@
             ref[s] = tall.T[take : take + RIM].astype(jnp.bfloat16)
 
 
-def rims_kernel(flags_ref, above_ref, below_ref, left_ref, right_ref, rims_ref):
+def rims_kernel(above_ref, below_ref, left_ref, right_ref, rims_ref):
     for n, ref in enumerate((above_ref, below_ref, left_ref, right_ref)):
-        keep = (flags_ref[n] > 0).astype(jnp.float32)
+        keep = inside("row" if n < 2 else "col", n % 2 == 1)
         part = (ref[...].astype(jnp.float32) * keep).astype(jnp.bfloat16)
         if n < 2:
             rims_ref[:, RIM * n : RIM * (n + 1), :512] = part
@@ -169,9 +175,9 @@
     return read
 
 
-def inner_kernel(flags_ref, tile_ref, above_ref, below_ref, columns_ref, rows_ref, inner_ref):
-    up = (flags_ref[0] > 0).astype(jnp.float32)
-    down = (flags_ref[1] > 0).astype(jnp.float32)
+def inner_kernel(tile_ref, above_ref, below_ref, columns_ref, rows_ref, inner_ref):
+    up = inside("row", False)
+    down = inside("row", True)
     columns, rows = columns_ref[...], rows_ref[...]
     for i in range(4):
         for s in range(2):
@@ -191,7 +197,7 @@
     return jnp.concatenate([both[RIM:], gap, both[:RIM]], axis=0).T
 
 
-def outer_kernel(flags_ref, tile_ref, rims_ref, inner_ref, columns_ref, rows_ref, outer_ref, rim_scr):
+def outer_kernel(tile_ref, rims_ref, inner_ref, columns_ref, rows_ref, outer_ref, rim_scr):
     columns, rows = columns_ref[...], rows_ref[...]
     for s in range(2):
         rim_scr[s] = side_blocks(rims_ref, s)
@@ -211,18 +217,21 @@
 def kernel(plan, *refs):
     fresh, pairs, at, cuts, span = plan
     refs = list(refs)
-    flags_ref = refs.pop(0)
     tile_refs = [refs.pop(0) for _ in cuts]
     rims_ref, inner_ref, outer_ref = refs.pop(0), refs.pop(0), refs.pop(0)
     if at:
+        given_ref = refs.pop(0)
         refs.pop(0)
     columns_ref, rows_ref, back_rows_ref, back_columns_ref = [refs.pop(0) for _ in range(4)]
-    out_ref, fresh_ref, rim_scr, half_scr, line_scr, wide_scr, sem = refs
-    live = (flags_ref[4] > 0).astype(jnp.float32)
+    out_ref = refs.pop(0)
+    side_ref = None if at else refs.pop(0)
+    fresh_ref, rim_scr, half_scr, line_scr, wide_scr, sem = refs
+    live = inside("gz", True)
     columns, rows = columns_ref[...], rows_ref[...]
     back_rows, back_columns = back_rows_ref[...], back_columns_ref[...]
-    for n, s in enumerate(fresh):
-        rim_scr[n] = side_blocks(rims_ref, s)
+    if not at:
+        rim_scr[0] = side_blocks(rims_ref, 0)
+        side_ref[...] = side_blocks(rims_ref, 1)
     for i in range(*span):
         for n, s in enumerate(fresh):
             parts = [(reader(rims_ref, s), -RIM, 0)]
@@ -230,7 +239,8 @@
                 parts.append((reader(ref, n), start, start + ref.shape[1]))
             parts.append((reader(rims_ref, s, RIM), 512, 512 + RIM))
             blocks = [window(parts, i, b) for b in range(4)]
-            rim = rim_scr[n, STRIDE * i : STRIDE * i + PATCH, :]
+            lines = slice(STRIDE * i, STRIDE * i + PATCH)
+            rim = given_ref[lines, :] if at else rim_scr[n, lines, :]
             for m, one in enumerate(spectra_of(blocks, rim, columns, rows, live, range(4))):
                 fresh_ref[n, i - span[0], m] = one
 
@@ -264,7 +274,6 @@
 
 
 IN_VMEM = pl.BlockSpec(memory_space=pltpu.VMEM)
-IN_SMEM = pl.BlockSpec(memory_space=pltpu.SMEM)
 ANYWHERE = pl.BlockSpec(memory_space=pl.ANY)
 PARAMS = pltpu.CompilerParams(vmem_limit_bytes=9 * 1024 * 1024)
 
@@ -273,21 +282,22 @@
     return pl.CostEstimate(flops=flops, bytes_accessed=1 << 20, transcendentals=0)
 
 
-def stage(flags, tiles, rims, inner, outer, earlier, consts, fresh, pairs, at, span=(0, 4)):
+def stage(tiles, rims, inner, outer, earlier, consts, fresh, pairs, at, span=(0, 4)):
     height = span[1] - span[0]
-    operands, aliases = [flags, *tiles.values(), rims, inner, outer], {}
-    specs = [IN_SMEM] + [IN_VMEM] * (len(operands) - 1)
+    operands, aliases = [*tiles.values(), rims, inner, outer], {}
+    specs = [IN_VMEM] * len(operands)
     if at:
-        aliases[len(operands)] = 0
-        operands.append(earlier)
-        specs.append(ANYWHERE)
+        aliases[len(operands) + 1] = 0
+        operands += earlier
+        specs += [IN_VMEM, ANYWHERE]
     operands += consts
     specs += [IN_VMEM] * len(consts)
     return pl.pallas_call(
         functools.partial(kernel, (fresh, pairs, at, tuple(tiles), span)),
         in_specs=specs,
-        out_specs=ANYWHERE,
-        out_shape=jax.ShapeDtypeStruct((4, 4, 4, 1024), jnp.float32),
+        out_specs=[ANYWHERE] if at else [ANYWHERE, IN_VMEM],
+        out_shape=[jax.ShapeDtypeStruct((4, 4, 4, 1024), jnp.float32)]
+        + ([] if at else [jax.ShapeDtypeStruct((640, 128), jnp.float32)]),
         input_output_aliases=aliases,
         scratch_shapes=[
             pltpu.VMEM((len(fresh), height, 4, PATCH, 256), jnp.bfloat16),
@@ -324,8 +334,6 @@
     consts = [jnp.asarray(t) for t in tables()]
     height, width = sections.shape[1:]
     row, col, gz = lax.axis_index("row"), lax.axis_index("col"), lax.axis_index("gz")
-    rows, cols, depth = lax.axis_size("row"), lax.axis_size("col"), lax.axis_size("gz")
-    flags = jnp.stack([row > 0, row < rows - 1, col > 0, col < cols - 1, gz < depth - 1]).astype(jnp.int32)
     bf = lambda *shape: jax.ShapeDtypeStruct(shape, jnp.bfloat16)
     top, bottom = cut(sections, [((0, 2), (0, RIM)), ((0, 2), (height - RIM, RIM))])
     first, upper = cut(sections, [((0, 1), (0, height)), ((1, 1), (0, CUT))])
@@ -335,61 +343,61 @@
     upper = ring(upper, "gz", -1)
 
     def around(operands):
-        flags, tile, above, below = operands
+        tile, above, below = operands
         low, high = pl.pallas_call(
             edges_kernel,
-            in_specs=[IN_SMEM] + [IN_VMEM] * 3,
+            in_specs=[IN_VMEM] * 3,
             out_specs=[IN_VMEM, IN_VMEM],
             out_shape=[bf(2, RIM, 640), bf(2, RIM, 640)],
             compiler_params=PARAMS,
-        )(flags, tile, above, below)
+        )(tile, above, below)
         left = ring(high, "col", 1)
         right = ring(low, "col", -1)
         inner = pl.pallas_call(
             inner_kernel,
-            in_specs=[IN_SMEM] + [IN_VMEM] * 5,
+            in_specs=[IN_VMEM] * 5,
             out_specs=IN_VMEM,
             out_shape=bf(2, 4, 2, PATCH, 256),
             compiler_params=PARAMS,
             cost_estimate=cost(10_000_000_000),
-        )(flags, tile, above, below, consts[0], consts[1])
+        )(tile, above, below, consts[0], consts[1])
         rims = pl.pallas_call(
             rims_kernel,
-            in_specs=[IN_SMEM] + [IN_VMEM] * 4,
+            in_specs=[IN_VMEM] * 4,
             out_specs=IN_VMEM,
             out_shape=bf(2, 4 * RIM, 640),
             compiler_params=PARAMS,
-        )(flags, above, below, left, right)
+        )(above, below, left, right)
         return rims, inner
 
     def nothing(operands):
         return jnp.zeros((2, 4 * RIM, 640), jnp.bfloat16), jnp.zeros((2, 4, 2, PATCH, 256), jnp.bfloat16)
 
     rims, inner = lax.cond(
-        row + col + gz < 99, around, nothing, (flags, sections, above, below)
+        row + col + gz < 99, around, nothing, (sections, above, below)
     )
     far = ring(rims, "gz", -1)
     outer = pl.pallas_call(
         outer_kernel,
-        in_specs=[IN_SMEM] + [IN_VMEM] * 5,
+        in_specs=[IN_VMEM] * 5,
         out_specs=IN_VMEM,
         out_shape=bf(2, 4, 2, PATCH, 256),
         scratch_shapes=[pltpu.VMEM((2, 640, 128), jnp.float32)],
         compiler_params=PARAMS,
         cost_estimate=cost(60_000_000_000),
-    )(flags, sections, rims, inner, consts[0], consts[1])
+    )(sections, rims, inner, consts[0], consts[1])
     later, outer = lax.optimization_barrier((sections, outer))
     lower = cut(later, [((1, 1), (a, b - a)) for a, b in zip(CUTS[:-1], CUTS[1:])])
     lower = [ring(part, "gz", -1) for part in lower]
     pairs = [(0, 1), (0, 2), (1, 2)]
-    result = stage(flags, {0: first}, far, inner, outer, None, consts, (0,), pairs, 0)
+    result, side = stage({0: first}, far, inner, outer, None, consts, (0,), pairs, 0)
     parts = {0: upper}
     spans = list(SPANS)
     if spans[0][0]:
-        result = stage(flags, parts, far, inner, outer, result, consts, (1,), [(1, 2)], 3, (0, spans[0][0]))
+        result, = stage(parts, far, inner, outer, (side, result), consts, (1,), [(1, 2)], 3, (0, spans[0][0]))
     for start, part, span in zip(CUTS, lower, spans):
         parts = {**parts, start: part}
-        result = stage(flags, parts, far, inner, outer, result, consts, (1,), [(1, 2)], 3, span)
+        result, = stage(parts, far, inner, outer, (side, result), consts, (1,), [(1, 2)], 3, span)
     return result.reshape(2, 2, 4, 4, OFF * OFF)
 
 

time: 39.4 us -> 36.9 us (0.937)
  Pallas kernels: 17.7 us -> 13.4 us
  waiting for transfers between devices: 2.61 us -> 4.29 us
    pallas_call x4, Pallas kernels: 5.9 us -> 3.64 us  [the longest x1 1.92 us: shards(): pl.pallas_call(outer_kernel, in_specs=[IN_VMEM] * 5, out_specs=IN_VMEM, o...]
    pallas_call x3, Pallas kernels: 10.5 us -> 8.43 us  [stage(): pl.pallas_call(functools.partial(kernel, (fresh, pairs, at, tuple(tiles),...]
    ppermute x8, waiting for transfers between devices: 2.61 us -> 4.29 us  [ring(): lax.ppermute(value, axis, [(n, (n + steps) % count) for n in range(count)])]
  transfers between devices with their start and end apart: 8 -> 8, of which waited for: 2 -> 3; matrix products, arithmetic and copies ran while one was open for 0% -> 0% of each run, Pallas kernels for 35% -> 28%
where the time goes in v4:
time: 36.9 us; the launch traced here: 36.5 us
  starting transfers between devices  18.5 us (50%)
  Pallas kernels  13.4 us (36%)
  waiting for transfers between devices  4.29 us (12%)
    ppermute x8, starting transfers between devices, ring(): lax.ppermute(value, axis, [(n, (n + steps) % count) for n in range(count)])  18.5 us
    pallas_call x3, Pallas kernels, stage(): pl.pallas_call(functools.partial(kernel, (fresh, pairs, at, tuple(tiles),...  8.43 us
    ppermute x8, waiting for transfers between devices, ring(): lax.ppermute(value, axis, [(n, (n + steps) % count) for n in range(count)])  4.29 us
    pallas_call x1, Pallas kernels, shards(): pl.pallas_call(outer_kernel, in_specs=[IN_VMEM] * 5, out_specs=IN_VMEM, o...  1.92 us
    pallas_call x1, Pallas kernels, around(): pl.pallas_call(inner_kernel, in_specs=[IN_VMEM] * 5, out_specs=IN_VMEM, o...  1.46 us
    pallas_call x3, Pallas kernels, cut(): pl.pallas_call(functools.partial(cut_kernel, parts), in_specs=[pl.BlockSp...  1.31 us
  transfers between devices with their start and end apart: 8, of which 3 were waited for; matrix products, arithmetic and copies ran while one was open for 0% of the time, Pallas kernels for 28%

profile of v4, /device:TPU:1, one launch (start us, length us, event | category | flops | bytes accessed | tf_op | source)
XLA Modules:
  0.0 36.5 jit_solution(7433215731116145830)
XLA Ops:
  0.0 0.9 %shard_map.56 = (bf16[2,16,512]{2,1,0:T(8,128)(2,1)S(1)}, bf16[2,16,512]{2,1,0:T(8,128)(2,1)S(1)}) custom-call(bf16[2,512,512]{2,1,0:T(8,128)(2,1)} %tile_ref.6), custom_call_target="tpu_custom_call" | custom-call | tf_op jit(solution)/shard_map/pallas_call | solution.py:316
  0.9 4.2 %collective-permute-start.3 = (bf16[2,16,512]{2,1,0:T(8,128)(2,1)S(1)}, bf16[2,16,512]{2,1,0:T(8,128)(2,1)S(1)}, u32[]{:S(2)}, u32[]{:S(2)}) collective-permute-start(bf16[2,16,512]{2,1,0:T(8,128)(2,1)S(1)} %get-tuple-element.33), channel_id=1, source_target_pairs={{0,8},{8,16},{16,24},{24,0},{1,9},{9,17},{17,25},{25,1},{2,10},{10... | collective-permute-start | bytes 98312 | tf_op jit(solution)/shard_map/ppermute | solution.py:330
  5.1 0.0 collective-permute-start.4
  5.1 0.0 copy-done.2
  5.1 0.2 shard_map.55
  5.4 2.8 %collective-permute-start.2 = (bf16[1,144,512]{2,1,0:T(8,128)(2,1)S(1)}, bf16[1,144,512]{2,1,0:T(8,128)(2,1)S(1)}, u32[]{:S(2)}, u32[]{:S(2)}) collective-permute-start(bf16[1,144,512]{2,1,0:T(8,128)(2,1)S(1)} %get-tuple-element.32), channel_id=1, source_target_pairs={{0,224},{32,0},{64,32},{96,64},{128,96},{160,128},{192,160},{224,1... | collective-permute-start | bytes 442376 | tf_op jit(solution)/shard_map/ppermute | solution.py:330
  8.2 1.2 %collective-permute-start.7 = (bf16[1,512,512]{2,1,0:T(8,128)(2,1)S(1)}, bf16[1,512,512]{2,1,0:T(8,128)(2,1)S(1)}, u32[]{:S(2)}, u32[]{:S(2)}) collective-permute-start(bf16[1,512,512]{2,1,0:T(8,128)(2,1)S(1)} %get-tuple-element.39), channel_id=1, source_target_pairs={{0,224},{32,0},{64,32},{96,64},{128,96},{160,128},{192,160},{224,1... | collective-permute-start | bytes 1572872 | tf_op jit(solution)/shard_map/ppermute | solution.py:330
  9.4 0.0 collective-permute-done.3
  9.4 0.6 %collective-permute-done.4 = bf16[2,16,512]{2,1,0:T(8,128)(2,1)S(1)} collective-permute-done((bf16[2,16,512]{2,1,0:T(8,128)(2,1)S(1)}, bf16[2,16,512]{2,1,0:T(8,128)(2,1)S(1)}, u32[]{:S(2)}, u32[]{:S(2)}) %collective-permute-start.4) | collective-permute-done | bytes 32800 | tf_op jit(solution)/shard_map/ppermute | solution.py:330
  10.0 0.0 copy-done.3
  10.0 0.0 copy-done.4
  10.0 7.5 %conditional.1 = (bf16[2,64,640]{2,1,0:T(8,128)(2,1)S(1)}, bf16[2,4,2,160,256]{4,3,2,1,0:T(8,128)(2,1)S(1)}) conditional(s32[]{:T(128)} %convert_element_type.3, () %tuple.14, (bf16[2,512,512]{2,1,0:T(8,128)(2,1)S(1)}, bf16[2,16,512]{2,1,0:T(8,128)(2,1)S(1)}, bf16[2,16,512]{2,1,0:T(8,128)(2,1)S(1)}, bf16[256,256]{1,0:T(8,128)(2,1)S(1)}, ...), branch_computations={%region_0.0_spmd, %region_1.0_spmd} | conditional | flops 10000000000 | bytes 1474580 | solution.py:376
  10.0 0.2 branch_1_fun.3
  10.2 1.7 %collective-permute-start = (bf16[2,16,640]{2,1,0:T(8,128)(2,1)S(1)}, bf16[2,16,640]{2,1,0:T(8,128)(2,1)S(1)}, u32[]{:S(2)}, u32[]{:S(2)}) collective-permute-start(bf16[2,16,640]{2,1,0:T(8,128)(2,1)S(1)} %get-tuple-element.18), channel_id=1, source_target_pairs={{0,1},{1,2},{2,3},{3,4},{4,5},{5,6},{6,7},{7,0},{8,9},{9,10},{10,1... | collective-permute-start | bytes 122888 | tf_op jit(solution)/shard_map/cond/branch_1_fun/ppermute | solution.py:330
  11.9 4.0 %collective-permute-start.1 = (bf16[2,16,640]{2,1,0:T(8,128)(2,1)S(1)}, bf16[2,16,640]{2,1,0:T(8,128)(2,1)S(1)}, u32[]{:S(2)}, u32[]{:S(2)}) collective-permute-start(bf16[2,16,640]{2,1,0:T(8,128)(2,1)S(1)} %get-tuple-element.19), channel_id=1, source_target_pairs={{0,7},{1,0},{2,1},{3,2},{4,3},{5,4},{6,5},{7,6},{8,15},{9,8},{10,9... | collective-permute-start | bytes 122888 | tf_op jit(solution)/shard_map/cond/branch_1_fun/ppermute | solution.py:330
  15.9 1.5 %branch_1_fun.5 = bf16[2,4,2,160,256]{4,3,2,1,0:T(8,128)(2,1)S(1)} custom-call(bf16[2,512,512]{2,1,0:T(8,128)(2,1)S(1)} %get-tuple-element.17.tile_ref, bf16[2,16,512]{2,1,0:T(8,128)(2,1)S(1)} %get-tuple-element.15.above_ref, bf16[2,16,512]{2,1,0:T(8,128)(2,1)S(1)} %get-tuple-element.16.below_ref, bf16[256,256]{1,0:T(8,128)(2,1)S(1)} %get-tuple-element.20.columns_ref, ...), custom_call_target="tpu_custom_call" | custom-call | flops 10000000000 | bytes 1048576 | tf_op jit(solution)/shard_map/cond/branch_1_fun/pallas_call | solution.py:356
  17.4 0.0 collective-permute-done.left_ref
  17.4 0.0 collective-permute-done.1.right_ref
  17.5 3.2 %collective-permute-start.6 = (bf16[2,64,640]{2,1,0:T(8,128)(2,1)S(1)}, bf16[2,64,640]{2,1,0:T(8,128)(2,1)S(1)}, u32[]{:S(2)}, u32[]{:S(2)}) collective-permute-start(bf16[2,64,640]{2,1,0:T(8,128)(2,1)S(1)} %get-tuple-element.35.rims_ref), channel_id=1, source_target_pairs={{0,224},{32,0},{64,32},{96,64},{128,96},{160,128},{192,160},{224,1... | collective-permute-start | bytes 491528 | tf_op jit(solution)/shard_map/ppermute | solution.py:330
  20.7 1.9 %shard_map.57.refs_3_.refs_4_ = bf16[2,4,2,160,256]{4,3,2,1,0:T(8,128)(2,1)S(1)} custom-call(bf16[2,512,512]{2,1,0:T(8,128)(2,1)S(1)} %copy-done.2, bf16[2,64,640]{2,1,0:T(8,128)(2,1)S(1)} %get-tuple-element.35.rims_ref, bf16[2,4,2,160,256]{4,3,2,1,0:T(8,128)(2,1)S(1)} %get-tuple-element.36.inner_ref.refs_2_.refs_3_, bf16[256,256]{1,0:T(8,128)(2,1)S(1)} %copy-done.3, ...), custom_call_target="tpu_custom_call" | custom-call | flops 60000002048 | bytes 1048576 | tf_op jit(solution)/shard_map/pallas_call | solution.py:380
  22.6 0.0 copy-start
  22.6 0.0 copy-start.1
  22.6 0.2 shard_map.58
  22.8 1.4 %collective-permute-start.5 = (bf16[1,368,512]{2,1,0:T(8,128)(2,1)S(1)}, bf16[1,368,512]{2,1,0:T(8,128)(2,1)S(1)}, u32[]{:S(2)}, u32[]{:S(2)}) collective-permute-start(bf16[1,368,512]{2,1,0:T(8,128)(2,1)S(1)} %shard_map.58), channel_id=1, source_target_pairs={{0,224},{32,0},{64,32},{96,64},{128,96},{160,128},{192,160},{224,1... | collective-permute-start | bytes 1130504 | tf_op jit(solution)/shard_map/ppermute | solution.py:330
  24.2 1.4 %collective-permute-done.6.refs_1_.refs_2_ = bf16[2,64,640]{2,1,0:T(8,128)(2,1)S(1)} collective-permute-done((bf16[2,64,640]{2,1,0:T(8,128)(2,1)S(1)}, bf16[2,64,640]{2,1,0:T(8,128)(2,1)S(1)}, u32[]{:S(2)}, u32[]{:S(2)}) %collective-permute-start.6) | collective-permute-done | bytes 163872 | tf_op jit(solution)/shard_map/ppermute | solution.py:330
  25.6 0.0 collective-permute-done.7.refs_0_
  25.6 0.0 copy-done.1
  25.6 4.2 %shard_map.59 = (f32[4,4,4,1024]{3,2,1,0:T(4,128)}, f32[640,128]{1,0:T(8,128)S(1)}) custom-call(bf16[1,512,512]{2,1,0:T(8,128)(2,1)S(1)} %collective-permute-done.7.refs_0_, bf16[2,64,640]{2,1,0:T(8,128)(2,1)S(1)} %collective-permute-done.6.refs_1_.refs_2_, bf16[2,4,2,160,256]{4,3,2,1,0:T(8,128)(2,1)S(1)} %get-tuple-element.36.inner_ref.refs_2_.refs_3_, ...), custom_call_target="tpu_custom_call" | custom-call | flops 60000002048 | bytes 1048576 | tf_op jit(solution)/shard_map/pallas_call | solution.py:295
  29.9 0.0 collective-permute-done.2.refs_0_
  29.9 1.8 %shard_map.60.refs_6_ = f32[4,4,4,1024]{3,2,1,0:T(4,128)} custom-call(bf16[1,144,512]{2,1,0:T(8,128)(2,1)S(1)} %collective-permute-done.2.refs_0_, bf16[2,64,640]{2,1,0:T(8,128)(2,1)S(1)} %collective-permute-done.6.refs_1_.refs_2_, bf16[2,4,2,160,256]{4,3,2,1,0:T(8,128)(2,1)S(1)} %get-tuple-element.36.inner_ref.refs_2_.refs_3_, ...), custom_call_target="tpu_custom_call", output_to_operand_aliasing={{}: (5, {})} | custom-call | flops 60000002048 | bytes 1048576 | tf_op jit(solution)/shard_map/pallas_call | solution.py:295
  31.7 2.3 %collective-permute-done.5.refs_1_ = bf16[1,368,512]{2,1,0:T(8,128)(2,1)S(1)} collective-permute-done((bf16[1,368,512]{2,1,0:T(8,128)(2,1)S(1)}, bf16[1,368,512]{2,1,0:T(8,128)(2,1)S(1)}, u32[]{:S(2)}, u32[]{:S(2)}) %collective-permute-start.5) | collective-permute-done | bytes 376864 | tf_op jit(solution)/shard_map/ppermute | solution.py:330
  33.9 2.4 %shard_map.61 = f32[4,4,4,1024]{3,2,1,0:T(4,128)} custom-call(bf16[1,144,512]{2,1,0:T(8,128)(2,1)S(1)} %collective-permute-done.2.refs_0_, bf16[1,368,512]{2,1,0:T(8,128)(2,1)S(1)} %collective-permute-done.5.refs_1_, bf16[2,64,640]{2,1,0:T(8,128)(2,1)S(1)} %collective-permute-done.6.refs_1_.refs_2_, ...), custom_call_target="tpu_custom_call", output_to_operand_aliasing={{}: (6, {})} | custom-call | flops 60000002048 | bytes 1048576 | tf_op jit(solution)/shard_map/pallas_call | solution.py:295
  (5 shorter events, 0.0 us)
Async XLA Ops:
  0.0 5.1 %copy-start.2 = (bf16[2,512,512]{2,1,0:T(8,128)(2,1)S(1)}, bf16[2,512,512]{2,1,0:T(8,128)(2,1)}, u32[]{:S(2)}) copy-start(bf16[2,512,512]{2,1,0:T(8,128)(2,1)} %tile_ref.6) | copy-start | bytes 3145732
  0.0 10.0 %copy-start.3 = (bf16[256,256]{1,0:T(8,128)(2,1)S(1)}, bf16[256,256]{1,0:T(8,128)(2,1)}, u32[]{:S(2)}) copy-start(bf16[256,256]{1,0:T(8,128)(2,1)} %constant.25.clone.columns_ref.refs_4_.refs_6_.refs_7_) | copy-start | bytes 393220
  0.0 10.0 %copy-start.4 = (bf16[160,160]{1,0:T(8,128)(2,1)S(1)}, bf16[160,160]{1,0:T(8,128)(2,1)}, u32[]{:S(2)}) copy-start(bf16[160,160]{1,0:T(8,128)(2,1)} %constant.26.clone.rows_ref.refs_5_.refs_7_.refs_8_) | copy-start | bytes 153604
  0.9 8.5 %collective-permute-start.3 = (bf16[2,16,512]{2,1,0:T(8,128)(2,1)S(1)}, bf16[2,16,512]{2,1,0:T(8,128)(2,1)S(1)}, u32[]{:S(2)}, u32[]{:S(2)}) collective-permute-start(bf16[2,16,512]{2,1,0:T(8,128)(2,1)S(1)} %get-tuple-element.33), channel_id=1, source_target_pairs={{0,8},{8,16},{16,24},{24,0},{1,9},{9,17},{17,25},{25,1},{2,10},{10... | collective-permute-start | bytes 98312 | tf_op jit(solution)/shard_map/ppermute | solution.py:330
  5.1 4.8 %collective-permute-start.4 = (bf16[2,16,512]{2,1,0:T(8,128)(2,1)S(1)}, bf16[2,16,512]{2,1,0:T(8,128)(2,1)S(1)}, u32[]{:S(2)}, u32[]{:S(2)}) collective-permute-start(bf16[2,16,512]{2,1,0:T(8,128)(2,1)S(1)} %get-tuple-element.34), channel_id=1, source_target_pairs={{0,24},{8,0},{16,8},{24,16},{1,25},{9,1},{17,9},{25,17},{2,26},{10... | collective-permute-start | bytes 98312 | tf_op jit(solution)/shard_map/ppermute | solution.py:330
  5.4 24.5 %collective-permute-start.2 = (bf16[1,144,512]{2,1,0:T(8,128)(2,1)S(1)}, bf16[1,144,512]{2,1,0:T(8,128)(2,1)S(1)}, u32[]{:S(2)}, u32[]{:S(2)}) collective-permute-start(bf16[1,144,512]{2,1,0:T(8,128)(2,1)S(1)} %get-tuple-element.32), channel_id=1, source_target_pairs={{0,224},{32,0},{64,32},{96,64},{128,96},{160,128},{192,160},{224,1... | collective-permute-start | bytes 442376 | tf_op jit(solution)/shard_map/ppermute | solution.py:330
  8.2 17.4 %collective-permute-start.7 = (bf16[1,512,512]{2,1,0:T(8,128)(2,1)S(1)}, bf16[1,512,512]{2,1,0:T(8,128)(2,1)S(1)}, u32[]{:S(2)}, u32[]{:S(2)}) collective-permute-start(bf16[1,512,512]{2,1,0:T(8,128)(2,1)S(1)} %get-tuple-element.39), channel_id=1, source_target_pairs={{0,224},{32,0},{64,32},{96,64},{128,96},{160,128},{192,160},{224,1... | collective-permute-start | bytes 1572872 | tf_op jit(solution)/shard_map/ppermute | solution.py:330
  10.2 7.2 %collective-permute-start = (bf16[2,16,640]{2,1,0:T(8,128)(2,1)S(1)}, bf16[2,16,640]{2,1,0:T(8,128)(2,1)S(1)}, u32[]{:S(2)}, u32[]{:S(2)}) collective-permute-start(bf16[2,16,640]{2,1,0:T(8,128)(2,1)S(1)} %get-tuple-element.18), channel_id=1, source_target_pairs={{0,1},{1,2},{2,3},{3,4},{4,5},{5,6},{6,7},{7,0},{8,9},{9,10},{10,1... | collective-permute-start | bytes 122888 | tf_op jit(solution)/shard_map/cond/branch_1_fun/ppermute | solution.py:330
  11.9 5.5 %collective-permute-start.1 = (bf16[2,16,640]{2,1,0:T(8,128)(2,1)S(1)}, bf16[2,16,640]{2,1,0:T(8,128)(2,1)S(1)}, u32[]{:S(2)}, u32[]{:S(2)}) collective-permute-start(bf16[2,16,640]{2,1,0:T(8,128)(2,1)S(1)} %get-tuple-element.19), channel_id=1, source_target_pairs={{0,7},{1,0},{2,1},{3,2},{4,3},{5,4},{6,5},{7,6},{8,15},{9,8},{10,9... | collective-permute-start | bytes 122888 | tf_op jit(solution)/shard_map/cond/branch_1_fun/ppermute | solution.py:330
  17.5 8.1 %collective-permute-start.6 = (bf16[2,64,640]{2,1,0:T(8,128)(2,1)S(1)}, bf16[2,64,640]{2,1,0:T(8,128)(2,1)S(1)}, u32[]{:S(2)}, u32[]{:S(2)}) collective-permute-start(bf16[2,64,640]{2,1,0:T(8,128)(2,1)S(1)} %get-tuple-element.35.rims_ref), channel_id=1, source_target_pairs={{0,224},{32,0},{64,32},{96,64},{128,96},{160,128},{192,160},{224,1... | collective-permute-start | bytes 491528 | tf_op jit(solution)/shard_map/ppermute | solution.py:330
  22.6 3.0 %copy-start = (bf16[1024,128]{1,0:T(8,128)(2,1)S(1)}, bf16[1024,128]{1,0:T(8,128)(2,1)}, u32[]{:S(2)}) copy-start(bf16[1024,128]{1,0:T(8,128)(2,1)} %constant.28.clone.refs_7_.refs_9_.refs_10_) | copy-start | bytes 786436
  22.6 3.0 %copy-start.1 = (bf16[32,160]{1,0:T(8,128)(2,1)S(1)}, bf16[32,160]{1,0:T(8,128)(2,1)}, u32[]{:S(2)}) copy-start(bf16[32,160]{1,0:T(8,128)(2,1)} %constant.27.clone.refs_6_.refs_8_.refs_9_) | copy-start | bytes 30724
  22.8 11.1 %collective-permute-start.5 = (bf16[1,368,512]{2,1,0:T(8,128)(2,1)S(1)}, bf16[1,368,512]{2,1,0:T(8,128)(2,1)S(1)}, u32[]{:S(2)}, u32[]{:S(2)}) collective-permute-start(bf16[1,368,512]{2,1,0:T(8,128)(2,1)S(1)} %shard_map.58), channel_id=1, source_target_pairs={{0,224},{32,0},{64,32},{96,64},{128,96},{160,128},{192,160},{224,1... | collective-permute-start | bytes 1130504 | tf_op jit(solution)/shard_map/ppermute | solution.py:330

commit v5 on v4

--- a/solution.py
+++ b/solution.py
@@ -66,8 +66,9 @@
 
 
 def with_top(special, rest):
-    top = lax.broadcasted_iota(jnp.int32, (8, 128), 0) == 0
-    return jnp.concatenate([jnp.where(top, special[:8], rest[:8]), rest[8:]], axis=0)
+    tile = 32 // special.dtype.itemsize
+    top = lax.broadcasted_iota(jnp.int32, (tile, 128), 0) == 0
+    return jnp.concatenate([jnp.where(top, special[:tile], rest[:tile]), rest[tile:]], axis=0)
 
 
 def spectra_of(blocks, rim, columns, rows, live, which):
@@ -102,8 +103,6 @@
 
 
 def half_back(left, right, back_rows):
-    left = left.astype(jnp.float32)
-    right = right.astype(jnp.float32)
     lr, li, rr, ri = left[:, :128], left[:, 128:], right[:, :128], right[:, 128:]
     real = lr * rr + li * ri
     imag = li * rr - lr * ri
@@ -111,7 +110,7 @@
     even = [with_top(pr, pr + mr), with_top(p_i, p_i + mi)]
     odd = [with_top(mr, mi - p_i), with_top(mi, pr - mr)]
     both = [jnp.concatenate(even, axis=1), jnp.concatenate(odd, axis=1)]
-    both = jnp.concatenate(both, axis=0).astype(jnp.bfloat16)
+    both = jnp.concatenate(both, axis=0)
     return jnp.dot(back_rows, both, preferred_element_type=jnp.float32)
 
 

time: 36.9 us -> 36.8 us (level)
  transfers between devices with their start and end apart: 8 -> 8, of which waited for: 3 -> 3; matrix products, arithmetic and copies ran while one was open for 0% -> 0% of each run, Pallas kernels for 28% -> 27%
where the time goes in v5:
time: 36.8 us; the launch traced here: 36.4 us
  starting transfers between devices  18.5 us (50%)
  Pallas kernels  13.1 us (36%)
  waiting for transfers between devices  4.47 us (12%)
    ppermute x8, starting transfers between devices, ring(): lax.ppermute(value, axis, [(n, (n + steps) % count) for n in range(count)])  18.5 us
    pallas_call x3, Pallas kernels, stage(): pl.pallas_call(functools.partial(kernel, (fresh, pairs, at, tuple(tiles),...  8.12 us
    ppermute x8, waiting for transfers between devices, ring(): lax.ppermute(value, axis, [(n, (n + steps) % count) for n in range(count)])  4.47 us
    pallas_call x1, Pallas kernels, shards(): pl.pallas_call(outer_kernel, in_specs=[IN_VMEM] * 5, out_specs=IN_VMEM, o...  1.92 us
    pallas_call x1, Pallas kernels, around(): pl.pallas_call(inner_kernel, in_specs=[IN_VMEM] * 5, out_specs=IN_VMEM, o...  1.46 us
    pallas_call x3, Pallas kernels, cut(): pl.pallas_call(functools.partial(cut_kernel, parts), in_specs=[pl.BlockSp...  1.31 us
  transfers between devices with their start and end apart: 8, of which 3 were waited for; matrix products, arithmetic and copies ran while one was open for 0% of the time, Pallas kernels for 27%

profile of v5, /device:TPU:1, one launch (start us, length us, event | category | flops | bytes accessed | tf_op | source)
XLA Modules:
  0.0 36.4 jit_solution(15599108712782975185)
XLA Ops:
  0.0 0.9 %shard_map.56 = (bf16[2,16,512]{2,1,0:T(8,128)(2,1)S(1)}, bf16[2,16,512]{2,1,0:T(8,128)(2,1)S(1)}) custom-call(bf16[2,512,512]{2,1,0:T(8,128)(2,1)} %tile_ref.6), custom_call_target="tpu_custom_call" | custom-call | tf_op jit(solution)/shard_map/pallas_call | solution.py:315
  0.9 4.2 %collective-permute-start.3 = (bf16[2,16,512]{2,1,0:T(8,128)(2,1)S(1)}, bf16[2,16,512]{2,1,0:T(8,128)(2,1)S(1)}, u32[]{:S(2)}, u32[]{:S(2)}) collective-permute-start(bf16[2,16,512]{2,1,0:T(8,128)(2,1)S(1)} %get-tuple-element.33), channel_id=1, source_target_pairs={{0,8},{8,16},{16,24},{24,0},{1,9},{9,17},{17,25},{25,1},{2,10},{10... | collective-permute-start | bytes 98312 | tf_op jit(solution)/shard_map/ppermute | solution.py:329
  5.1 0.0 collective-permute-start.4
  5.1 0.0 copy-done.2
  5.1 0.2 shard_map.55
  5.4 2.8 %collective-permute-start.2 = (bf16[1,144,512]{2,1,0:T(8,128)(2,1)S(1)}, bf16[1,144,512]{2,1,0:T(8,128)(2,1)S(1)}, u32[]{:S(2)}, u32[]{:S(2)}) collective-permute-start(bf16[1,144,512]{2,1,0:T(8,128)(2,1)S(1)} %get-tuple-element.32), channel_id=1, source_target_pairs={{0,224},{32,0},{64,32},{96,64},{128,96},{160,128},{192,160},{224,1... | collective-permute-start | bytes 442376 | tf_op jit(solution)/shard_map/ppermute | solution.py:329
  8.2 1.2 %collective-permute-start.7 = (bf16[1,512,512]{2,1,0:T(8,128)(2,1)S(1)}, bf16[1,512,512]{2,1,0:T(8,128)(2,1)S(1)}, u32[]{:S(2)}, u32[]{:S(2)}) collective-permute-start(bf16[1,512,512]{2,1,0:T(8,128)(2,1)S(1)} %get-tuple-element.39), channel_id=1, source_target_pairs={{0,224},{32,0},{64,32},{96,64},{128,96},{160,128},{192,160},{224,1... | collective-permute-start | bytes 1572872 | tf_op jit(solution)/shard_map/ppermute | solution.py:329
  9.4 0.0 collective-permute-done.3
  9.4 0.6 %collective-permute-done.4 = bf16[2,16,512]{2,1,0:T(8,128)(2,1)S(1)} collective-permute-done((bf16[2,16,512]{2,1,0:T(8,128)(2,1)S(1)}, bf16[2,16,512]{2,1,0:T(8,128)(2,1)S(1)}, u32[]{:S(2)}, u32[]{:S(2)}) %collective-permute-start.4) | collective-permute-done | bytes 32800 | tf_op jit(solution)/shard_map/ppermute | solution.py:329
  10.0 0.0 copy-done.3
  10.0 0.0 copy-done.4
  10.0 7.5 %conditional.1 = (bf16[2,64,640]{2,1,0:T(8,128)(2,1)S(1)}, bf16[2,4,2,160,256]{4,3,2,1,0:T(8,128)(2,1)S(1)}) conditional(s32[]{:T(128)} %convert_element_type.3, () %tuple.14, (bf16[2,512,512]{2,1,0:T(8,128)(2,1)S(1)}, bf16[2,16,512]{2,1,0:T(8,128)(2,1)S(1)}, bf16[2,16,512]{2,1,0:T(8,128)(2,1)S(1)}, bf16[256,256]{1,0:T(8,128)(2,1)S(1)}, ...), branch_computations={%region_0.0_spmd, %region_1.0_spmd} | conditional | flops 10000000000 | bytes 1474580 | solution.py:375
  10.0 0.2 branch_1_fun.3
  10.2 1.7 %collective-permute-start = (bf16[2,16,640]{2,1,0:T(8,128)(2,1)S(1)}, bf16[2,16,640]{2,1,0:T(8,128)(2,1)S(1)}, u32[]{:S(2)}, u32[]{:S(2)}) collective-permute-start(bf16[2,16,640]{2,1,0:T(8,128)(2,1)S(1)} %get-tuple-element.18), channel_id=1, source_target_pairs={{0,1},{1,2},{2,3},{3,4},{4,5},{5,6},{6,7},{7,0},{8,9},{9,10},{10,1... | collective-permute-start | bytes 122888 | tf_op jit(solution)/shard_map/cond/branch_1_fun/ppermute | solution.py:329
  11.9 4.0 %collective-permute-start.1 = (bf16[2,16,640]{2,1,0:T(8,128)(2,1)S(1)}, bf16[2,16,640]{2,1,0:T(8,128)(2,1)S(1)}, u32[]{:S(2)}, u32[]{:S(2)}) collective-permute-start(bf16[2,16,640]{2,1,0:T(8,128)(2,1)S(1)} %get-tuple-element.19), channel_id=1, source_target_pairs={{0,7},{1,0},{2,1},{3,2},{4,3},{5,4},{6,5},{7,6},{8,15},{9,8},{10,9... | collective-permute-start | bytes 122888 | tf_op jit(solution)/shard_map/cond/branch_1_fun/ppermute | solution.py:329
  15.9 1.5 %branch_1_fun.5 = bf16[2,4,2,160,256]{4,3,2,1,0:T(8,128)(2,1)S(1)} custom-call(bf16[2,512,512]{2,1,0:T(8,128)(2,1)S(1)} %get-tuple-element.17.tile_ref, bf16[2,16,512]{2,1,0:T(8,128)(2,1)S(1)} %get-tuple-element.15.above_ref, bf16[2,16,512]{2,1,0:T(8,128)(2,1)S(1)} %get-tuple-element.16.below_ref, bf16[256,256]{1,0:T(8,128)(2,1)S(1)} %get-tuple-element.20.columns_ref, ...), custom_call_target="tpu_custom_call" | custom-call | flops 10000000000 | bytes 1048576 | tf_op jit(solution)/shard_map/cond/branch_1_fun/pallas_call | solution.py:355
  17.4 0.0 collective-permute-done.left_ref
  17.4 0.0 collective-permute-done.1.right_ref
  17.5 3.2 %collective-permute-start.6 = (bf16[2,64,640]{2,1,0:T(8,128)(2,1)S(1)}, bf16[2,64,640]{2,1,0:T(8,128)(2,1)S(1)}, u32[]{:S(2)}, u32[]{:S(2)}) collective-permute-start(bf16[2,64,640]{2,1,0:T(8,128)(2,1)S(1)} %get-tuple-element.35.rims_ref), channel_id=1, source_target_pairs={{0,224},{32,0},{64,32},{96,64},{128,96},{160,128},{192,160},{224,1... | collective-permute-start | bytes 491528 | tf_op jit(solution)/shard_map/ppermute | solution.py:329
  20.7 1.9 %shard_map.57.refs_3_.refs_4_ = bf16[2,4,2,160,256]{4,3,2,1,0:T(8,128)(2,1)S(1)} custom-call(bf16[2,512,512]{2,1,0:T(8,128)(2,1)S(1)} %copy-done.2, bf16[2,64,640]{2,1,0:T(8,128)(2,1)S(1)} %get-tuple-element.35.rims_ref, bf16[2,4,2,160,256]{4,3,2,1,0:T(8,128)(2,1)S(1)} %get-tuple-element.36.inner_ref.refs_2_.refs_3_, bf16[256,256]{1,0:T(8,128)(2,1)S(1)} %copy-done.3, ...), custom_call_target="tpu_custom_call" | custom-call | flops 60000002048 | bytes 1048576 | tf_op jit(solution)/shard_map/pallas_call | solution.py:379
  22.6 0.0 copy-start
  22.6 0.0 copy-start.1
  22.6 0.2 shard_map.58
  22.8 1.4 %collective-permute-start.5 = (bf16[1,368,512]{2,1,0:T(8,128)(2,1)S(1)}, bf16[1,368,512]{2,1,0:T(8,128)(2,1)S(1)}, u32[]{:S(2)}, u32[]{:S(2)}) collective-permute-start(bf16[1,368,512]{2,1,0:T(8,128)(2,1)S(1)} %shard_map.58), channel_id=1, source_target_pairs={{0,224},{32,0},{64,32},{96,64},{128,96},{160,128},{192,160},{224,1... | collective-permute-start | bytes 1130504 | tf_op jit(solution)/shard_map/ppermute | solution.py:329
  24.2 1.4 %collective-permute-done.6.refs_1_.refs_2_ = bf16[2,64,640]{2,1,0:T(8,128)(2,1)S(1)} collective-permute-done((bf16[2,64,640]{2,1,0:T(8,128)(2,1)S(1)}, bf16[2,64,640]{2,1,0:T(8,128)(2,1)S(1)}, u32[]{:S(2)}, u32[]{:S(2)}) %collective-permute-start.6) | collective-permute-done | bytes 163872 | tf_op jit(solution)/shard_map/ppermute | solution.py:329
  25.6 0.0 collective-permute-done.7.refs_0_
  25.6 0.0 copy-done
  25.6 4.1 %shard_map.59 = (f32[4,4,4,1024]{3,2,1,0:T(4,128)}, f32[640,128]{1,0:T(8,128)S(1)}) custom-call(bf16[1,512,512]{2,1,0:T(8,128)(2,1)S(1)} %collective-permute-done.7.refs_0_, bf16[2,64,640]{2,1,0:T(8,128)(2,1)S(1)} %collective-permute-done.6.refs_1_.refs_2_, bf16[2,4,2,160,256]{4,3,2,1,0:T(8,128)(2,1)S(1)} %get-tuple-element.36.inner_ref.refs_2_.refs_3_, ...), custom_call_target="tpu_custom_call" | custom-call | flops 60000002048 | bytes 1048576 | tf_op jit(solution)/shard_map/pallas_call | solution.py:294
  29.7 0.0 collective-permute-done.2.refs_0_
  29.7 1.8 %shard_map.60.refs_6_ = f32[4,4,4,1024]{3,2,1,0:T(4,128)} custom-call(bf16[1,144,512]{2,1,0:T(8,128)(2,1)S(1)} %collective-permute-done.2.refs_0_, bf16[2,64,640]{2,1,0:T(8,128)(2,1)S(1)} %collective-permute-done.6.refs_1_.refs_2_, bf16[2,4,2,160,256]{4,3,2,1,0:T(8,128)(2,1)S(1)} %get-tuple-element.36.inner_ref.refs_2_.refs_3_, ...), custom_call_target="tpu_custom_call", output_to_operand_aliasing={{}: (5, {})} | custom-call | flops 60000002048 | bytes 1048576 | tf_op jit(solution)/shard_map/pallas_call | solution.py:294
  31.5 2.5 %collective-permute-done.5.refs_1_ = bf16[1,368,512]{2,1,0:T(8,128)(2,1)S(1)} collective-permute-done((bf16[1,368,512]{2,1,0:T(8,128)(2,1)S(1)}, bf16[1,368,512]{2,1,0:T(8,128)(2,1)S(1)}, u32[]{:S(2)}, u32[]{:S(2)}) %collective-permute-start.5) | collective-permute-done | bytes 376864 | tf_op jit(solution)/shard_map/ppermute | solution.py:329
  33.9 2.3 %shard_map.61 = f32[4,4,4,1024]{3,2,1,0:T(4,128)} custom-call(bf16[1,144,512]{2,1,0:T(8,128)(2,1)S(1)} %collective-permute-done.2.refs_0_, bf16[1,368,512]{2,1,0:T(8,128)(2,1)S(1)} %collective-permute-done.5.refs_1_, bf16[2,64,640]{2,1,0:T(8,128)(2,1)S(1)} %collective-permute-done.6.refs_1_.refs_2_, ...), custom_call_target="tpu_custom_call", output_to_operand_aliasing={{}: (6, {})} | custom-call | flops 60000002048 | bytes 1048576 | tf_op jit(solution)/shard_map/pallas_call | solution.py:294
  (5 shorter events, 0.0 us)
Async XLA Ops:
  0.0 5.1 %copy-start.2 = (bf16[2,512,512]{2,1,0:T(8,128)(2,1)S(1)}, bf16[2,512,512]{2,1,0:T(8,128)(2,1)}, u32[]{:S(2)}) copy-start(bf16[2,512,512]{2,1,0:T(8,128)(2,1)} %tile_ref.6) | copy-start | bytes 3145732
  0.0 10.0 %copy-start.3 = (bf16[256,256]{1,0:T(8,128)(2,1)S(1)}, bf16[256,256]{1,0:T(8,128)(2,1)}, u32[]{:S(2)}) copy-start(bf16[256,256]{1,0:T(8,128)(2,1)} %constant.25.clone.columns_ref.refs_4_.refs_6_.refs_7_) | copy-start | bytes 393220
  0.0 10.0 %copy-start.4 = (bf16[160,160]{1,0:T(8,128)(2,1)S(1)}, bf16[160,160]{1,0:T(8,128)(2,1)}, u32[]{:S(2)}) copy-start(bf16[160,160]{1,0:T(8,128)(2,1)} %constant.26.clone.rows_ref.refs_5_.refs_7_.refs_8_) | copy-start | bytes 153604
  0.9 8.5 %collective-permute-start.3 = (bf16[2,16,512]{2,1,0:T(8,128)(2,1)S(1)}, bf16[2,16,512]{2,1,0:T(8,128)(2,1)S(1)}, u32[]{:S(2)}, u32[]{:S(2)}) collective-permute-start(bf16[2,16,512]{2,1,0:T(8,128)(2,1)S(1)} %get-tuple-element.33), channel_id=1, source_target_pairs={{0,8},{8,16},{16,24},{24,0},{1,9},{9,17},{17,25},{25,1},{2,10},{10... | collective-permute-start | bytes 98312 | tf_op jit(solution)/shard_map/ppermute | solution.py:329
  5.1 4.8 %collective-permute-start.4 = (bf16[2,16,512]{2,1,0:T(8,128)(2,1)S(1)}, bf16[2,16,512]{2,1,0:T(8,128)(2,1)S(1)}, u32[]{:S(2)}, u32[]{:S(2)}) collective-permute-start(bf16[2,16,512]{2,1,0:T(8,128)(2,1)S(1)} %get-tuple-element.34), channel_id=1, source_target_pairs={{0,24},{8,0},{16,8},{24,16},{1,25},{9,1},{17,9},{25,17},{2,26},{10... | collective-permute-start | bytes 98312 | tf_op jit(solution)/shard_map/ppermute | solution.py:329
  5.4 24.3 %collective-permute-start.2 = (bf16[1,144,512]{2,1,0:T(8,128)(2,1)S(1)}, bf16[1,144,512]{2,1,0:T(8,128)(2,1)S(1)}, u32[]{:S(2)}, u32[]{:S(2)}) collective-permute-start(bf16[1,144,512]{2,1,0:T(8,128)(2,1)S(1)} %get-tuple-element.32), channel_id=1, source_target_pairs={{0,224},{32,0},{64,32},{96,64},{128,96},{160,128},{192,160},{224,1... | collective-permute-start | bytes 442376 | tf_op jit(solution)/shard_map/ppermute | solution.py:329
  8.2 17.4 %collective-permute-start.7 = (bf16[1,512,512]{2,1,0:T(8,128)(2,1)S(1)}, bf16[1,512,512]{2,1,0:T(8,128)(2,1)S(1)}, u32[]{:S(2)}, u32[]{:S(2)}) collective-permute-start(bf16[1,512,512]{2,1,0:T(8,128)(2,1)S(1)} %get-tuple-element.39), channel_id=1, source_target_pairs={{0,224},{32,0},{64,32},{96,64},{128,96},{160,128},{192,160},{224,1... | collective-permute-start | bytes 1572872 | tf_op jit(solution)/shard_map/ppermute | solution.py:329
  10.2 7.2 %collective-permute-start = (bf16[2,16,640]{2,1,0:T(8,128)(2,1)S(1)}, bf16[2,16,640]{2,1,0:T(8,128)(2,1)S(1)}, u32[]{:S(2)}, u32[]{:S(2)}) collective-permute-start(bf16[2,16,640]{2,1,0:T(8,128)(2,1)S(1)} %get-tuple-element.18), channel_id=1, source_target_pairs={{0,1},{1,2},{2,3},{3,4},{4,5},{5,6},{6,7},{7,0},{8,9},{9,10},{10,1... | collective-permute-start | bytes 122888 | tf_op jit(solution)/shard_map/cond/branch_1_fun/ppermute | solution.py:329
  11.9 5.5 %collective-permute-start.1 = (bf16[2,16,640]{2,1,0:T(8,128)(2,1)S(1)}, bf16[2,16,640]{2,1,0:T(8,128)(2,1)S(1)}, u32[]{:S(2)}, u32[]{:S(2)}) collective-permute-start(bf16[2,16,640]{2,1,0:T(8,128)(2,1)S(1)} %get-tuple-element.19), channel_id=1, source_target_pairs={{0,7},{1,0},{2,1},{3,2},{4,3},{5,4},{6,5},{7,6},{8,15},{9,8},{10,9... | collective-permute-start | bytes 122888 | tf_op jit(solution)/shard_map/cond/branch_1_fun/ppermute | solution.py:329
  17.5 8.1 %collective-permute-start.6 = (bf16[2,64,640]{2,1,0:T(8,128)(2,1)S(1)}, bf16[2,64,640]{2,1,0:T(8,128)(2,1)S(1)}, u32[]{:S(2)}, u32[]{:S(2)}) collective-permute-start(bf16[2,64,640]{2,1,0:T(8,128)(2,1)S(1)} %get-tuple-element.35.rims_ref), channel_id=1, source_target_pairs={{0,224},{32,0},{64,32},{96,64},{128,96},{160,128},{192,160},{224,1... | collective-permute-start | bytes 491528 | tf_op jit(solution)/shard_map/ppermute | solution.py:329
  22.6 3.0 %copy-start = (bf16[1024,128]{1,0:T(8,128)(2,1)S(1)}, bf16[1024,128]{1,0:T(8,128)(2,1)}, u32[]{:S(2)}) copy-start(bf16[1024,128]{1,0:T(8,128)(2,1)} %constant.28.clone.refs_7_.refs_9_.refs_10_) | copy-start | bytes 786436
  22.6 3.0 %copy-start.1 = (bf16[32,160]{1,0:T(8,128)(2,1)S(1)}, bf16[32,160]{1,0:T(8,128)(2,1)}, u32[]{:S(2)}) copy-start(bf16[32,160]{1,0:T(8,128)(2,1)} %constant.27.clone.refs_6_.refs_8_.refs_9_) | copy-start | bytes 30724
  22.8 11.1 %collective-permute-start.5 = (bf16[1,368,512]{2,1,0:T(8,128)(2,1)S(1)}, bf16[1,368,512]{2,1,0:T(8,128)(2,1)S(1)}, u32[]{:S(2)}, u32[]{:S(2)}) collective-permute-start(bf16[1,368,512]{2,1,0:T(8,128)(2,1)S(1)} %shard_map.58), channel_id=1, source_target_pairs={{0,224},{32,0},{64,32},{96,64},{128,96},{160,128},{192,160},{224,1... | collective-permute-start | bytes 1130504 | tf_op jit(solution)/shard_map/ppermute | solution.py:329
